TPU v7x, 32 devices: a whole 2x2x4 slice. The times are simulated.
32 devices in a mesh: rep: 4 (over z), fsdp: 8 (over y, x, core).
Axes of the slice: x: 2, y: 2, z: 4, core: 2. Of those that a mesh axis runs over, the one named last changes fastest.
Arguments:
- features: bfloat16 [384, 28, 28, 128], P(('rep', 'fsdp')), may hold values from -6 to 6
- labels: int32 [384], P(('rep', 'fsdp')), may hold values from 0 to 999
- counts: int32 [4, 8], P('rep', 'fsdp'), may hold values from 1 to 12, as said below
- tables: int32 [2, 196, 49], replicated, may hold values from 0 to 195, as said below
- conv_weight: float32 [1152, 256], P('fsdp'), may hold values from -0.1875 to 0.1875
- qkv_weight: float32 [2, 256, 768], P(None, 'fsdp'), may hold values from -0.375 to 0.375
- proj_weight: float32 [2, 256, 256], P(None, 'fsdp'), may hold values from -1 to 1
- up_weight: float32 [2, 256, 768], P(None, 'fsdp'), may hold values from -0.375 to 0.375
- down_weight: float32 [2, 768, 256], P(None, 'fsdp'), may hold values from -0.21875 to 0.21875
- head_weight: float32 [256, 1000], P('fsdp'), may hold values from -4 to 4
- conv_mom: float32 [1152, 256], P('fsdp'), may hold values from -0.0234375 to 0.0234375
- qkv_mom: float32 [2, 256, 768], P(None, 'fsdp'), may hold values from -0.0234375 to 0.0234375
- proj_mom: float32 [2, 256, 256], P(None, 'fsdp'), may hold values from -0.0234375 to 0.0234375
- up_mom: float32 [2, 256, 768], P(None, 'fsdp'), may hold values from -0.0234375 to 0.0234375
- down_mom: float32 [2, 768, 256], P(None, 'fsdp'), may hold values from -0.0234375 to 0.0234375
- head_mom: float32 [256, 1000], P('fsdp'), may hold values from -0.3125 to 0.3125
- conv_err: float32 [4, 1152, 256], P('rep', 'fsdp'), may hold values from -0.0234375 to 0.0234375
- qkv_err: float32 [4, 2, 256, 768], P('rep', None, 'fsdp'), may hold values from -0.0234375 to 0.0234375
- proj_err: float32 [4, 2, 256, 256], P('rep', None, 'fsdp'), may hold values from -0.0234375 to 0.0234375
- up_err: float32 [4, 2, 256, 768], P('rep', None, 'fsdp'), may hold values from -0.0234375 to 0.0234375
- down_err: float32 [4, 2, 768, 256], P('rep', None, 'fsdp'), may hold values from -0.0234375 to 0.0234375
- head_err: float32 [4, 256, 1000], P('rep', 'fsdp'), may hold values from -0.3125 to 0.3125
- conv_fac: float32 [256, 8], replicated, may hold values from -5 to 5
- qkv_fac: float32 [2, 768, 8], replicated, may hold values from -5 to 5
- proj_fac: float32 [2, 256, 8], replicated, may hold values from -5 to 5
- up_fac: float32 [2, 768, 8], replicated, may hold values from -5 to 5
- down_fac: float32 [2, 256, 8], replicated, may hold values from -5 to 5
- head_fac: float32 [1000, 8], replicated, may hold values from -5 to 5
- small_params: float32 [10616], replicated
- small_mom: float32 [10616], replicated, may hold values from -0.3125 to 0.3125
Outputs:
- loss_sum: float32 [], replicated
- item_count: float32 [], replicated
- new_conv_weight: float32 [1152, 256], P('fsdp')
- new_qkv_weight: float32 [2, 256, 768], P(None, 'fsdp')
- new_proj_weight: float32 [2, 256, 256], P(None, 'fsdp')
- new_up_weight: float32 [2, 256, 768], P(None, 'fsdp')
- new_down_weight: float32 [2, 768, 256], P(None, 'fsdp')
- new_head_weight: float32 [256, 1000], P('fsdp')
- new_conv_mom: float32 [1152, 256], P('fsdp')
- new_qkv_mom: float32 [2, 256, 768], P(None, 'fsdp')
- new_proj_mom: float32 [2, 256, 256], P(None, 'fsdp')
- new_up_mom: float32 [2, 256, 768], P(None, 'fsdp')
- new_down_mom: float32 [2, 768, 256], P(None, 'fsdp')
- new_head_mom: float32 [256, 1000], P('fsdp')
- new_conv_err: float32 [4, 1152, 256], P('rep', 'fsdp')
- new_qkv_err: float32 [4, 2, 256, 768], P('rep', None, 'fsdp')
- new_proj_err: float32 [4, 2, 256, 256], P('rep', None, 'fsdp')
- new_up_err: float32 [4, 2, 256, 768], P('rep', None, 'fsdp')
- new_down_err: float32 [4, 2, 768, 256], P('rep', None, 'fsdp')
- new_head_err: float32 [4, 256, 1000], P('rep', 'fsdp')
- new_conv_fac: float32 [256, 8], replicated
- new_qkv_fac: float32 [2, 768, 8], replicated
- new_proj_fac: float32 [2, 256, 8], replicated
- new_up_fac: float32 [2, 768, 8], replicated
- new_down_fac: float32 [2, 256, 8], replicated
- new_head_fac: float32 [1000, 8], replicated
- new_small_params: float32 [10616], replicated
- new_small_mom: float32 [10616], replicated
Inputs may be any that keep to these rules, and one draw needn't show every extreme that they name: counts: live items of each device; the last device of both axes holds 12. `tables`: row q of layer l lists, in some order, the 49 cells of the 7 x 7 neighbourhood of cell q (cells numbered row by row on the 14 x 14 grid) with dilation 1 + (l mod 2), the window moved inside the grid at its rims.
All inputs are finite; a program needn't handle non-finite values.
Results may differ from a plain program's by a relative error of at most 0.012.
The roundings to bfloat16 on the way count: a program that leaves them out, or rounds other values in their place, can miss the bound.
Values may be sent and summed in bfloat16 or wider, within the bound.
No kernel may reach another device: no remote copies, remote signals or barrier semaphores. Data moves between devices by JAX's collectives and lax.ppermute only.
A program may use at most 320 MiB of HBM per device.

v0:
```python
import jax
import jax.numpy as jnp
from jax import lax
from jax.sharding import PartitionSpec as P

D = 256
HEADS = 8
HEAD = 32
FF = 768
CLASSES = 1000
CIN = 128
GRID = 14
KER = 7
LAYERS = 2
PIX = 196
RB = 169


EPSILON = 1e-05
MASKED = -1000000000.0
MOMENTUM = 0.9
LEARN_RATE = 16.0
SMALL_RATE = 4.0
PRECISE = lax.Precision.HIGHEST


def segments():
    pieces = [("bias", D), ("gain", D), ("bias", D)]
    for layer_idx in range(LAYERS):
        pieces += [
            ("gain", D),
            ("bias", D),
            ("bias", D),
            ("bias", D),
            ("bias", D),
            ("gain", D),
            ("bias", D),
            ("bias", D),
            ("bias", FF),
            ("table", HEADS * RB),
        ]
    return pieces + [("gain", D), ("bias", D), ("bias", CLASSES)]


def unpack(vector):
    pieces, offset = ([], 0)
    for seg_kind, length in segments():
        pieces.append(vector[offset : offset + length])
        offset += length
    return pieces


def layer_norm(values, gain, shift):
    centred = values - jnp.mean(values, axis=-1, keepdims=True)
    variance = jnp.mean(centred * centred, axis=-1, keepdims=True)
    return centred * lax.rsqrt(variance + EPSILON) * gain + shift


def patches_of(images):
    padded = jnp.pad(images, ((0, 0), (1, 1), (1, 1), (0, 0)))
    blocks = padded.reshape(images.shape[0], GRID + 1, 2, GRID + 1, 2, images.shape[-1])
    return jnp.concatenate(
        [
            blocks[
                :,
                row_off // 2 : row_off // 2 + GRID,
                row_off % 2,
                col_off // 2 : col_off // 2 + GRID,
                col_off % 2,
                :,
            ]
            for row_off in range(3)
            for col_off in range(3)
        ],
        axis=-1,
    )


def neighbour_maps(tables):
    cell_ids = jnp.arange(PIX, dtype=jnp.int32)
    key_maps, rel_maps = ([], [])
    for layer_idx in range(LAYERS):
        dilation = 1 + layer_idx % 2
        table_now = tables[layer_idx]
        row_step = table_now // GRID // dilation - (cell_ids // GRID // dilation)[:, None] + KER - 1
        col_step = table_now % GRID // dilation - (cell_ids % GRID // dilation)[:, None] + KER - 1
        rel_index = row_step * (2 * KER - 1) + col_step
        key_maps.append((table_now[:, :, None] == cell_ids[None, None, :]).astype(jnp.float32))
        rel_maps.append(
            (rel_index[:, :, None] == jnp.arange(RB, dtype=jnp.int32)[None, None, :]).astype(
                jnp.float32
            )
        )
    return (key_maps, rel_maps)


def dense_bias(key_map, rel_map, rel_table):
    chosen = jnp.einsum("qjr,hr->hqj", rel_map, rel_table.reshape(HEADS, RB), precision=PRECISE)
    spread = jnp.einsum("qjk,hqj->hqk", key_map, chosen, precision=PRECISE)
    inside = jnp.sum(key_map, axis=1) > 0.5
    return jnp.where(inside[None], spread, MASKED)


def attend_scores(joined, bias_map):
    return (
        jnp.einsum("nhqe,nhke->nhqk", joined[0], joined[1], preferred_element_type=jnp.float32)
        * HEAD ** (-0.5)
        + bias_map
    )


def sum_rows(values):
    return jnp.sum(values.astype(jnp.float32), axis=(0, 1))


def layer_forward(hidden, weights, vectors, bias_map):
    qkv_w, proj_w, up_w, down_w = weights
    (
        gain_one,
        shift_one,
        bias_query,
        bias_value,
        bias_proj,
        gain_two,
        shift_two,
        bias_down,
        bias_up,
        rel_table,
    ) = vectors
    qkv_heads = qkv_w.reshape(D, 3, HEADS, HEAD)
    joined_bias = jnp.stack([bias_query, jnp.zeros_like(bias_query), bias_value]).reshape(
        3, 1, HEADS, 1, HEAD
    )
    normed_one = layer_norm(hidden, gain_one, shift_one).astype(jnp.bfloat16)
    joined = (
        jnp.einsum("npd,dshe->snhpe", normed_one, qkv_heads, preferred_element_type=jnp.float32)
        + joined_bias
    ).astype(jnp.bfloat16)
    scores = attend_scores(joined, bias_map)
    row_peak = jnp.max(scores, axis=-1, keepdims=True)
    exp_terms = jnp.exp(scores - row_peak)
    row_total = jnp.sum(exp_terms, axis=-1, keepdims=True)
    attn_probs = (exp_terms / row_total).astype(jnp.bfloat16)
    mixed_out = jnp.einsum(
        "nhqk,nhke->nhqe", attn_probs, joined[2], preferred_element_type=jnp.float32
    ).astype(jnp.bfloat16)
    after_attn = hidden + (
        jnp.einsum(
            "nhpe,hed->npd",
            mixed_out,
            proj_w.reshape(HEADS, HEAD, D),
            preferred_element_type=jnp.float32,
        )
        + bias_proj
    )
    normed_two = layer_norm(after_attn, gain_two, shift_two).astype(jnp.bfloat16)
    pre_act = (
        jnp.einsum("npd,df->npf", normed_two, up_w, preferred_element_type=jnp.float32) + bias_up
    )
    active = jax.nn.gelu(pre_act, approximate=False).astype(jnp.bfloat16)
    output = after_attn + (
        jnp.einsum("npf,fd->npd", active, down_w, preferred_element_type=jnp.float32) + bias_down
    )
    return (
        output,
        (
            hidden,
            normed_one,
            joined,
            row_peak + jnp.log(row_total),
            mixed_out,
            after_attn,
            normed_two,
            pre_act,
            active,
        ),
    )


def layer_backward(d_output, cache, weights, vectors, bias_map, key_map, rel_map):
    hidden, normed_one, joined, log_total, mixed_out, after_attn, normed_two, pre_act, active = (
        cache
    )
    qkv_w, proj_w, up_w, down_w = weights
    (
        gain_one,
        shift_one,
        bias_query,
        bias_value,
        bias_proj,
        gain_two,
        shift_two,
        bias_down,
        bias_up,
        rel_table,
    ) = vectors
    d_branch = d_output.astype(jnp.bfloat16)
    g_down = jnp.einsum("npf,npd->fd", active, d_branch, preferred_element_type=jnp.float32)
    g_bias_down = sum_rows(d_branch)
    d_active = jnp.einsum("npd,fd->npf", d_branch, down_w, preferred_element_type=jnp.float32)
    d_pre = jax.vjp(lambda x: jax.nn.gelu(x, approximate=False), pre_act)[1](d_active)[0].astype(
        jnp.bfloat16
    )
    g_bias_up = sum_rows(d_pre)
    g_up = jnp.einsum("npd,npf->df", normed_two, d_pre, preferred_element_type=jnp.float32)
    d_normed_two = jnp.einsum("npf,df->npd", d_pre, up_w, preferred_element_type=jnp.float32)
    d_after_norm, g_gain_two, g_shift_two = jax.vjp(layer_norm, after_attn, gain_two, shift_two)[1](
        d_normed_two
    )
    d_after = d_output + d_after_norm
    d_proj = d_after.astype(jnp.bfloat16)
    g_bias_proj = sum_rows(d_proj)
    g_proj = jnp.einsum(
        "nhpe,npd->hed", mixed_out, d_proj, preferred_element_type=jnp.float32
    ).reshape(D, D)
    d_mixed = jnp.einsum(
        "npd,hed->nhpe", d_proj, proj_w.reshape(HEADS, HEAD, D), preferred_element_type=jnp.float32
    ).astype(jnp.bfloat16)
    probs_full = jnp.exp(attend_scores(joined, bias_map) - log_total)
    d_probs = jnp.einsum("nhqe,nhke->nhqk", d_mixed, joined[2], preferred_element_type=jnp.float32)
    g_values = jnp.einsum(
        "nhqk,nhqe->nhke",
        probs_full.astype(jnp.bfloat16),
        d_mixed,
        preferred_element_type=jnp.float32,
    )
    d_scores = (
        probs_full * (d_probs - jnp.sum(d_probs * probs_full, axis=-1, keepdims=True))
    ).astype(jnp.bfloat16)
    g_bias_map = jnp.sum(d_scores.astype(jnp.float32), axis=0)
    d_chosen = jnp.einsum("qjk,hqk->hqj", key_map, g_bias_map, precision=PRECISE)
    g_rel = jnp.einsum("qjr,hqj->hr", rel_map, d_chosen, precision=PRECISE).reshape(-1)
    g_queries = jnp.einsum(
        "nhqk,nhke->nhqe", d_scores, joined[1], preferred_element_type=jnp.float32
    ) * HEAD ** (-0.5)
    g_keys = jnp.einsum(
        "nhqk,nhqe->nhke", d_scores, joined[0], preferred_element_type=jnp.float32
    ) * HEAD ** (-0.5)
    d_joined = jnp.stack([g_queries, g_keys, g_values]).astype(jnp.bfloat16)
    g_joined_bias = jnp.sum(d_joined.astype(jnp.float32), axis=(1, 3)).reshape(3, D)
    g_qkv = jnp.einsum(
        "npd,snhpe->dshe", normed_one, d_joined, preferred_element_type=jnp.float32
    ).reshape(D, 3 * D)
    d_normed_one = jnp.einsum(
        "snhpe,dshe->npd",
        d_joined,
        qkv_w.reshape(D, 3, HEADS, HEAD),
        preferred_element_type=jnp.float32,
    )
    d_hidden_norm, g_gain_one, g_shift_one = jax.vjp(layer_norm, hidden, gain_one, shift_one)[1](
        d_normed_one
    )
    vector_grads = [
        g_gain_one,
        g_shift_one,
        g_joined_bias[0],
        g_joined_bias[2],
        g_bias_proj,
        g_gain_two,
        g_shift_two,
        g_bias_down,
        g_bias_up,
        g_rel,
    ]
    return (d_after + d_hidden_norm, (g_qkv, g_proj, g_up, g_down), vector_grads)


def orthonormal(product, gram_mat):
    lower_tri = jnp.linalg.cholesky(gram_mat)
    return jnp.swapaxes(
        jax.scipy.linalg.solve_triangular(lower_tri, jnp.swapaxes(product, 1, 2), lower=True), 1, 2
    )


def body(
    features,
    labels,
    counts,
    tables,
    conv_weight,
    qkv_weight,
    proj_weight,
    up_weight,
    down_weight,
    head_weight,
    conv_mom,
    qkv_mom,
    proj_mom,
    up_mom,
    down_mom,
    head_mom,
    conv_err,
    qkv_err,
    proj_err,
    up_err,
    down_err,
    head_err,
    conv_fac,
    qkv_fac,
    proj_fac,
    up_fac,
    down_fac,
    head_fac,
    small_params,
    small_mom,
):
    slot_count = features.shape[0]
    live_mask = (jnp.arange(slot_count, dtype=jnp.int32) < counts[0, 0]).astype(jnp.float32)
    pieces = unpack(small_params)
    key_maps, rel_maps = neighbour_maps(tables)
    layer_vectors = [
        pieces[3 + 10 * layer_idx : 13 + 10 * layer_idx] for layer_idx in range(LAYERS)
    ]
    bias_maps = [
        dense_bias(key_maps[layer_idx], rel_maps[layer_idx], layer_vectors[layer_idx][9])
        for layer_idx in range(LAYERS)
    ]
    conv_full, head_full = (
        lax.all_gather(conv_weight.astype(jnp.bfloat16), "fsdp", axis=0, tiled=True),
        lax.all_gather(head_weight.astype(jnp.bfloat16), "fsdp", axis=0, tiled=True),
    )
    patches = patches_of(features).reshape(slot_count, PIX, 9 * CIN)
    conv_out = (
        jnp.einsum("npc,cd->npd", patches, conv_full, preferred_element_type=jnp.float32)
        + pieces[0]
    )
    hidden = layer_norm(conv_out, pieces[1], pieces[2])
    caches, gathered = ([], [])
    for layer_idx in range(LAYERS):
        layer_w = (
            lax.all_gather(qkv_weight[layer_idx].astype(jnp.bfloat16), "fsdp", axis=0, tiled=True),
            lax.all_gather(proj_weight[layer_idx].astype(jnp.bfloat16), "fsdp", axis=0, tiled=True),
            lax.all_gather(up_weight[layer_idx].astype(jnp.bfloat16), "fsdp", axis=0, tiled=True),
            lax.all_gather(down_weight[layer_idx].astype(jnp.bfloat16), "fsdp", axis=0, tiled=True),
        )
        hidden, cache = layer_forward(
            hidden, layer_w, layer_vectors[layer_idx], bias_maps[layer_idx]
        )
        caches.append(cache)
        gathered.append(layer_w)
    final_norm = layer_norm(hidden, pieces[-3], pieces[-2])
    pooled = jnp.mean(final_norm, axis=1).astype(jnp.bfloat16)
    logits = jnp.dot(pooled, head_full, preferred_element_type=jnp.float32) + pieces[-1]
    row_peak = jnp.max(logits, axis=-1, keepdims=True)
    log_total = row_peak + jnp.log(jnp.sum(jnp.exp(logits - row_peak), axis=-1, keepdims=True))
    onehot = (labels[:, None] == jnp.arange(CLASSES, dtype=jnp.int32)[None, :]).astype(jnp.float32)
    losses = log_total[:, 0] - jnp.sum(logits * onehot, axis=-1)
    loss_sum, item_count = lax.psum(
        (jnp.sum(live_mask * losses), jnp.sum(live_mask)), ("rep", "fsdp")
    )
    inverse = 1.0 / item_count
    d_logits = ((jnp.exp(logits - log_total) - onehot) * (inverse * live_mask)[:, None]).astype(
        jnp.bfloat16
    )
    g_head = jnp.einsum("nd,nc->dc", pooled, d_logits, preferred_element_type=jnp.float32)
    g_bias_head = jnp.sum(d_logits.astype(jnp.float32), axis=0)
    d_pooled = jnp.einsum("nc,dc->nd", d_logits, head_full, preferred_element_type=jnp.float32)
    d_final = jnp.broadcast_to(d_pooled[:, None, :] / PIX, final_norm.shape)
    d_hidden, g_gain_final, g_shift_final = jax.vjp(layer_norm, hidden, pieces[-3], pieces[-2])[1](
        d_final
    )
    matrix_parts = [None] * LAYERS
    vector_parts = [None] * LAYERS
    for layer_idx in reversed(range(LAYERS)):
        layer_w = (
            lax.all_gather(qkv_weight[layer_idx].astype(jnp.bfloat16), "fsdp", axis=0, tiled=True),
            lax.all_gather(proj_weight[layer_idx].astype(jnp.bfloat16), "fsdp", axis=0, tiled=True),
            lax.all_gather(up_weight[layer_idx].astype(jnp.bfloat16), "fsdp", axis=0, tiled=True),
            lax.all_gather(down_weight[layer_idx].astype(jnp.bfloat16), "fsdp", axis=0, tiled=True),
        )
        d_hidden, layer_mats, vector_parts[layer_idx] = layer_backward(
            d_hidden,
            caches[layer_idx],
            layer_w,
            layer_vectors[layer_idx],
            bias_maps[layer_idx],
            key_maps[layer_idx],
            rel_maps[layer_idx],
        )
        matrix_parts[layer_idx] = layer_mats
    d_conv, g_gain_conv, g_shift_conv = jax.vjp(layer_norm, conv_out, pieces[1], pieces[2])[1](
        d_hidden
    )
    d_conv = d_conv.astype(jnp.bfloat16)
    g_conv = jnp.einsum("npc,npd->cd", patches, d_conv, preferred_element_type=jnp.float32)
    g_bias_conv = sum_rows(d_conv)
    stacks = [
        jnp.stack([matrix_parts[layer_idx][which] for layer_idx in range(LAYERS)])
        for which in range(4)
    ]
    reduced = (
        lax.psum_scatter(stacks[0], "fsdp", scatter_dimension=1, tiled=True),
        lax.psum_scatter(stacks[1], "fsdp", scatter_dimension=1, tiled=True),
        lax.psum_scatter(stacks[2], "fsdp", scatter_dimension=1, tiled=True),
        lax.psum_scatter(stacks[3], "fsdp", scatter_dimension=1, tiled=True),
        lax.psum_scatter(g_conv, "fsdp", scatter_dimension=0, tiled=True),
        lax.psum_scatter(g_head, "fsdp", scatter_dimension=0, tiled=True),
    )
    mat_shards = [reduced[0], reduced[1], reduced[2], reduced[3]]
    conv_shard, head_shard = (reduced[4], reduced[5])
    small_list = [g_bias_conv, g_gain_conv, g_shift_conv]
    for layer_idx in range(LAYERS):
        small_list += vector_parts[layer_idx]
    small_grad = jnp.concatenate(small_list + [g_gain_final, g_shift_final, g_bias_head])
    grads_all = [conv_shard[None]] + mat_shards + [head_shard[None]]
    errors = [conv_err, qkv_err[0], proj_err[0], up_err[0], down_err[0], head_err]
    factors = [conv_fac[None], qkv_fac, proj_fac, up_fac, down_fac, head_fac[None]]
    weights_all = [
        conv_weight[None],
        qkv_weight,
        proj_weight,
        up_weight,
        down_weight,
        head_weight[None],
    ]
    moms_all = [conv_mom[None], qkv_mom, proj_mom, up_mom, down_mom, head_mom[None]]
    merged = [g + e for g, e in zip(grads_all, errors)]
    local_p = [jnp.einsum("bio,bok->bik", m, f, precision=PRECISE) for m, f in zip(merged, factors)]
    p_sum = lax.psum(
        (local_p[0], local_p[1], local_p[2], local_p[3], local_p[4], local_p[5]), "rep"
    )
    local_gram = [jnp.einsum("bik,bil->bkl", p, p, precision=PRECISE) for p in p_sum]
    grams = lax.psum(
        (local_gram[0], local_gram[1], local_gram[2], local_gram[3], local_gram[4], local_gram[5]),
        "fsdp",
    )
    bases = [orthonormal(p, g) for p, g in zip(p_sum, grams)]
    local_q = [jnp.einsum("bio,bik->bok", m, b, precision=PRECISE) for m, b in zip(merged, bases)]
    q_rows = lax.psum(
        (local_q[0], local_q[1], local_q[2], local_q[3], local_q[4], local_q[5], small_grad), "fsdp"
    )
    q_sums = lax.psum(
        (q_rows[0], q_rows[1], q_rows[2], q_rows[3], q_rows[4], q_rows[5], q_rows[6]), "rep"
    )
    new_weights, new_moms, new_errs = ([], [], [])
    for which in range(6):
        new_errs.append(
            merged[which]
            - jnp.einsum("bik,bok->bio", bases[which], q_rows[which], precision=PRECISE)
        )
        new_mom = MOMENTUM * moms_all[which] + jnp.einsum(
            "bik,bok->bio", bases[which], q_sums[which], precision=PRECISE
        )
        new_moms.append(new_mom)
        new_weights.append(weights_all[which] - LEARN_RATE * new_mom)
    new_small_mom = MOMENTUM * small_mom + q_sums[6]
    new_small = small_params - SMALL_RATE * new_small_mom
    return (
        loss_sum,
        item_count,
        new_weights[0][0],
        new_weights[1],
        new_weights[2],
        new_weights[3],
        new_weights[4],
        new_weights[5][0],
        new_moms[0][0],
        new_moms[1],
        new_moms[2],
        new_moms[3],
        new_moms[4],
        new_moms[5][0],
        new_errs[0],
        new_errs[1][None],
        new_errs[2][None],
        new_errs[3][None],
        new_errs[4][None],
        new_errs[5],
        q_sums[0][0],
        q_sums[1],
        q_sums[2],
        q_sums[3],
        q_sums[4],
        q_sums[5][0],
        new_small,
        new_small_mom,
    )


def solution(mesh):
    placed = (
        P(("rep", "fsdp"), None, None, None),
        P(("rep", "fsdp")),
        P("rep", "fsdp"),
        P(),
        P("fsdp", None),
        P(None, "fsdp", None),
        P(None, "fsdp", None),
        P(None, "fsdp", None),
        P(None, "fsdp", None),
        P("fsdp", None),
        P("fsdp", None),
        P(None, "fsdp", None),
        P(None, "fsdp", None),
        P(None, "fsdp", None),
        P(None, "fsdp", None),
        P("fsdp", None),
        P("rep", "fsdp", None),
        P("rep", None, "fsdp", None),
        P("rep", None, "fsdp", None),
        P("rep", None, "fsdp", None),
        P("rep", None, "fsdp", None),
        P("rep", "fsdp", None),
        P(),
        P(),
        P(),
        P(),
        P(),
        P(),
        P(),
        P(),
    )
    return jax.shard_map(
        body,
        mesh=mesh,
        in_specs=placed,
        out_specs=(
            P(),
            P(),
            P("fsdp", None),
            P(None, "fsdp", None),
            P(None, "fsdp", None),
            P(None, "fsdp", None),
            P(None, "fsdp", None),
            P("fsdp", None),
            P("fsdp", None),
            P(None, "fsdp", None),
            P(None, "fsdp", None),
            P(None, "fsdp", None),
            P(None, "fsdp", None),
            P("fsdp", None),
            P("rep", "fsdp", None),
            P("rep", None, "fsdp", None),
            P("rep", None, "fsdp", None),
            P("rep", None, "fsdp", None),
            P("rep", None, "fsdp", None),
            P("rep", "fsdp", None),
            P(),
            P(),
            P(),
            P(),
            P(),
            P(),
            P(),
            P(),
        ),
        check_vma=False,
    )
```

profile of v0, /device:TPU:0, one launch (start us, length us, event | category | flops | bytes accessed | tf_op | source)
XLA Modules:
  0.0 917.3 jit_solution(12734472672849209635)
XLA Ops:
  23.9 11.7 %all-gather.1 = bf16[1,256,256]{2,1,0:T(8,128)(2,1)} all-gather(bf16[1,32,256]{2,1,0:T(8,128)(2,1)S(1)} %get-tuple-element.160), channel_id=3, replica_groups=mesh['rep'=4,'fsdp'=8] {'fsdp'}, dimensions={1}, use_global_device_ids=true | all-gather | bytes 147456 | tf_op jit(solution)/shard_map/all_gather | solution.py:332
  41.2 9.5 %all-gather.4 = bf16[1,256,768]{2,1,0:T(8,128)(2,1)S(1)} all-gather(bf16[1,32,768]{2,1,0:T(8,128)(2,1)S(1)} %get-tuple-element.132), channel_id=6, replica_groups=mesh['rep'=4,'fsdp'=8] {'fsdp'}, dimensions={1}, use_global_device_ids=true | all-gather | bytes 442368 | tf_op jit(solution)/shard_map/all_gather | solution.py:331
  51.7 9.6 %all-gather.3 = bf16[1,768,256]{2,1,0:T(8,128)(2,1)} all-gather(bf16[1,96,256]{2,1,0:T(8,128)(2,1)S(1)} %get-tuple-element.129), channel_id=5, replica_groups=mesh['rep'=4,'fsdp'=8] {'fsdp'}, dimensions={1}, use_global_device_ids=true | all-gather | bytes 442368 | tf_op jit(solution)/shard_map/all_gather | solution.py:334
  61.3 10.5 %all-gather.2 = bf16[1,256,768]{2,1,0:T(8,128)(2,1)} all-gather(bf16[1,32,768]{2,1,0:T(8,128)(2,1)S(1)} %get-tuple-element.131), channel_id=4, replica_groups=mesh['rep'=4,'fsdp'=8] {'fsdp'}, dimensions={1}, use_global_device_ids=true | all-gather | bytes 442368 | tf_op jit(solution)/shard_map/all_gather | solution.py:333
  71.7 9.2 %all-gather = bf16[1,256,768]{2,1,0:T(8,128)(2,1)S(1)} all-gather(bf16[1,32,768]{2,1,0:T(8,128)(2,1)S(1)} %get-tuple-element.133), channel_id=2, replica_groups=mesh['rep'=4,'fsdp'=8] {'fsdp'}, dimensions={1}, use_global_device_ids=true | all-gather | bytes 442368 | tf_op jit(solution)/shard_map/all_gather | solution.py:331
  88.8 11.1 %all_gather.38 = bf16[1152,256]{1,0:T(8,128)(2,1)} all-gather(bf16[144,256]{1,0:T(8,128)(2,1)S(1)} %convert_element_type.193), channel_id=1, replica_groups=mesh['rep'=4,'fsdp'=8] {'fsdp'}, dimensions={0}, use_global_device_ids=true | all-gather | bytes 663552 | tf_op jit(solution)/shard_map/all_gather | solution.py:319
  123.5 32.2 %slice_reduce_fusion = (bf16[12,14,14,128]{3,2,1,0:T(8,128)(2,1)}, bf16[12,14,14,128]{3,2,1,0:T(8,128)(2,1)}, bf16[12,14,14,128]{3,2,1,0:T(8,128)(2,1)}, bf16[12...) fusion(bf16[12,15,2,15,2,128]{5,4,3,2,1,0:T(2,128)(2,1)S(1)} %r, ...), kind=kLoop, calls=%fused_computation.213 | loop fusion | bytes 10838016 | tf_op jit(solution)/shard_map/slice | solution.py:64
  178.3 8.4 fusion.227
  186.7 11.2 %fusion = f32[12,8,196]{2,1,0:T(8,128)S(1)} fusion(f32[12,8,196,196]{2,3,1,0:T(8,128)} %get-tuple-element.174, f32[12,8,196]{2,1,0:T(8,128)S(1)} %get-tuple-element.173), kind=kLoop, calls=%fused_computation.14 | loop fusion | flops 7357056 | bytes 14902272 | tf_op jit(solution)/shard_map/reduce_sum | solution.py:142
  198.0 9.0 fusion.52
  214.0 17.7 %multiply_convert_fusion.3 = (bf16[12,196,768]{2,1,0:T(8,128)(2,1)S(1)}, f32[12,196,768]{2,1,0:T(8,128)}) fusion(f32[12,196,768]{2,1,0:T(8,128)S(1)} %get-tuple-element.177, f32[768]{0:T(1024)S(1)} %copy-done.173, u16[196,768]{1,0:T(8,128)(2,1)S(1)} %get-tuple-element.34, u16[196,768]{1,0:T(8,128)(2,1)S(1)} %get-tuple-element.33), kind=kLoop, calls=%fused_computation.72 | loop fusion | flops 128249856 | bytes 18668544 | tf_op jit(solution)/shard_map/convert_element_type | solution.py:160
  236.8 8.8 fusion.230
  245.6 11.2 %fusion.1 = f32[12,8,196]{2,1,0:T(8,128)S(1)} fusion(f32[12,8,196,196]{2,3,1,0:T(8,128)} %get-tuple-element.181, f32[12,8,196]{2,1,0:T(8,128)S(1)} %get-tuple-element.180), kind=kLoop, calls=%fused_computation.15 | loop fusion | flops 7357056 | bytes 14902272 | tf_op jit(solution)/shard_map/reduce_sum | solution.py:142
  256.9 8.9 fusion.51
  267.1 8.4 all-gather.5
  275.6 9.4 %all-gather.7 = bf16[1,768,256]{2,1,0:T(8,128)(2,1)S(1)} all-gather(bf16[1,96,256]{2,1,0:T(8,128)(2,1)S(1)} %copy-done.118), channel_id=9, replica_groups=mesh['rep'=4,'fsdp'=8] {'fsdp'}, dimensions={1}, use_global_device_ids=true | all-gather | bytes 442368 | tf_op jit(solution)/shard_map/all_gather | solution.py:334
  285.0 8.8 all-gather.6
  293.7 10.1 %all_gather.47 = bf16[256,1000]{1,0:T(8,128)(2,1)S(1)} all-gather(bf16[32,1000]{1,0:T(8,128)(2,1)S(1)} %convert_element_type.219), channel_id=1, replica_groups=mesh['rep'=4,'fsdp'=8] {'fsdp'}, dimensions={0}, use_global_device_ids=true | all-gather | bytes 576000 | tf_op jit(solution)/shard_map/all_gather | solution.py:320
  309.8 17.7 %multiply_convert_fusion.2 = (bf16[12,196,768]{2,1,0:T(8,128)(2,1)S(1)}, f32[12,196,768]{2,1,0:T(8,128)}) fusion(f32[12,196,768]{2,1,0:T(8,128)S(1)} %get-tuple-element.184, f32[768]{0:T(1024)S(1)} %copy-done.175, u16[196,768]{1,0:T(8,128)(2,1)S(1)} %get-tuple-element.32, u16[196,768]{1,0:T(8,128)(2,1)S(1)} %get-tuple-element.31), kind=kLoop, calls=%fused_computation.59 | loop fusion | flops 128249856 | bytes 18668544 | tf_op jit(solution)/shard_map/convert_element_type | solution.py:160
  333.0 39.9 %all-reduce.1 = (f32[]{:T(128)}, f32[]{:T(128)}) all-reduce(f32[]{:T(128)} %get-tuple-element.120, f32[]{:T(128)} %convert_reduce_fusion.14), channel_id=1, replica_groups=mesh['rep'=4,'fsdp'=8] {'rep','fsdp'}, use_global_device_ids=true, to_apply=%region_23.24 | all-reduce | flops 2 | bytes 16 | tf_op jit(solution)/shard_map/psum | solution.py:348
  407.2 14.7 %multiply_reduce_fusion.1 = (f32[12,8,196]{2,1,0:T(8,128)S(1)}, f32[12,8,196,196]{2,3,1,0:T(8,128)}) fusion(f32[12,8,196,196]{2,3,1,0:T(8,128)} %get-tuple-element.181, f32[12,8,196]{2,1,0:T(8,128)S(1)} %log_add_fusion.1, bf16[3,12,8,196,32]{3,4,2,0,1:T(8,128)(2,1)} %copy-done.20, bf16[12,196,8,32]{1,3,2,0:T(8,128)(2,1)} %convolution_convert_fusion.1), kind=kOutput, calls=%fused_computation.6 | convolution fusion | flops 247072896 | bytes 37708800 | tf_op jit(solution)/shard_map/nhqe,nhke->nhqk/dot_general | solution.py:220
  421.9 20.6 %convert_reduce_fusion = (f32[8,196,196]{1,2,0:T(8,128)}, bf16[12,8,196,196]{2,3,1,0:T(8,128)(2,1)}) fusion(f32[12,8,196,196]{2,3,1,0:T(8,128)} %get-tuple-element.191, f32[12,8,196]{2,1,0:T(8,128)S(1)} %get-tuple-element.190, f32[12,8,196,196]{2,3,1,0:T(8,128)} %get-tuple-element.181, f32[12,8,196]{2,1,0:T(8,128)S(1)} %log_add_fusion.1), kind=kLoop, calls=%fused_computation | loop fusion | flops 21820288 | bytes 38259200 | tf_op jit(solution)/shard_map/reduce_sum | solution.py:230
  485.3 9.9 %fusion.69 = bf16[1,12,8,196,32]{3,4,2,1,0:T(8,128)(2,1)} fusion(bf16[12,196,8,32]{1,3,2,0:T(8,128)(2,1)S(1)} %convolution_convert_fusion, f32[12,8,196,196]{2,3,1,0:T(8,128)} %get-tuple-element.174, f32[12,8,196]{2,1,0:T(8,128)S(1)} %log_add_fusion), kind=kOutput, calls=%fused_computation.190 | convolution fusion | flops 244005888 | bytes 17235456 | tf_op jit(solution)/shard_map/nhqk,nhqe->nhke/dot_general | solution.py:221
  495.3 12.7 %multiply_reduce_fusion = (f32[12,8,196]{2,1,0:T(8,128)S(1)}, f32[12,8,196,196]{2,3,1,0:T(8,128)}) fusion(f32[12,8,196,196]{2,3,1,0:T(8,128)} %get-tuple-element.174, f32[12,8,196]{2,1,0:T(8,128)S(1)} %log_add_fusion, bf16[3,12,8,196,32]{3,4,2,0,1:T(8,128)(2,1)S(1)} %bitcast.579, bf16[12,196,8,32]{1,3,2,0:T(8,128)(2,1)S(1)} %convolution_convert_fusion), kind=kOutput, calls=%fused_computation.3 | convolution fusion | flops 247072896 | bytes 32822784 | tf_op jit(solution)/shard_map/nhqe,nhke->nhqk/dot_general | solution.py:220
  508.0 20.5 %convert_reduce_fusion.1 = (f32[8,196,196]{1,2,0:T(8,128)}, bf16[12,8,196,196]{2,3,1,0:T(8,128)(2,1)}) fusion(f32[12,8,196,196]{2,3,1,0:T(8,128)} %get-tuple-element.195, f32[12,8,196]{2,1,0:T(8,128)S(1)} %get-tuple-element.194, f32[12,8,196,196]{2,3,1,0:T(8,128)} %get-tuple-element.174, f32[12,8,196]{2,1,0:T(8,128)S(1)} %log_add_fusion), kind=kLoop, calls=%fused_computation.1 | loop fusion | flops 21820288 | bytes 38259200 | tf_op jit(solution)/shard_map/reduce_sum | solution.py:230
  528.5 8.4 fusion.68
  643.6 40.4 %reduce-scatter.13.cloned.1.call-done = f32[2,32,768]{2,1,0:T(8,128)} async-done(((f32[2,256,768]{2,1,0:T(8,128)}), f32[2,32,768]{2,1,0:T(8,128)}) %reduce-scatter.13.cloned.1.call-update) | async-done | bytes 196624 | tf_op jit(solution)/shard_map/reduce_scatter | solution.py:394
  685.3 40.3 %reduce-scatter.9.cloned.1.call-done = f32[2,32,768]{2,1,0:T(8,128)} async-done(((f32[2,256,768]{2,1,0:T(8,128)}), f32[2,32,768]{2,1,0:T(8,128)}) %reduce-scatter.9.cloned.1.call-update) | async-done | bytes 196624 | tf_op jit(solution)/shard_map/reduce_scatter | solution.py:392
  726.9 19.7 %all-reduce.5 = (f32[1,144,8]{1,2,0:T(8,128)S(1)}, f32[2,32,8]{1,2,0:T(8,128)S(1)}, f32[2,96,8]{1,2,0:T(8,128)S(1)}, f32[2,32,8]{1,2,0:T(8,128)S(1)}, f32[2,32,8]{1,2,0:T(8,128)S(1)}, /*index=5*/f32[1,32,8]{1,2,0:T(8,128)S(1)}) all-reduce(f32[1,144,8]{1,2,0:T(8,128)S(1)} %convolution_bitcast_fusion.9, ...), channel_id=1, replica_groups=mesh['rep'=4,'fsdp'=8] {'rep'}, use_global_device_ids=true, to_apply=%region_41.42 | all-reduce | flops 4480 | bytes 35840 | tf_op jit(solution)/shard_map/psum | solution.py:419
  747.5 22.7 %all-reduce.3 = (f32[1,8,8]{1,2,0:T(8,128)S(1)}, f32[2,8,8]{1,2,0:T(8,128)S(1)}, f32[2,8,8]{1,2,0:T(8,128)S(1)}, f32[2,8,8]{1,2,0:T(8,128)S(1)}, f32[2,8,8]{1,2,0:T(8,128)S(1)}, /*index=5*/f32[1,8,8]{1,2,0:T(8,128)S(1)}) all-reduce(f32[1,8,8]{1,2,0:T(8,128)S(1)} %convolution_bitcast_fusion.12, ...), channel_id=1, replica_groups=mesh['rep'=4,'fsdp'=8] {'fsdp'}, use_global_device_ids=true, to_apply=%region_42.43 | all-reduce | flops 640 | bytes 5120 | tf_op jit(solution)/shard_map/psum | solution.py:423
  793.9 51.5 %all-reduce.9.cloned.1.call-done = (f32[1,256,8]{1,2,0:T(8,128)}, f32[2,768,8]{1,2,0:T(8,128)}, f32[2,256,8]{1,2,0:T(8,128)}, f32[2,768,8]{1,2,0:T(8,128)}, f32[...) async-done(((f32[1,256,8]{1,2,0:T(8,128)}, f32[2,768,8]{1,2,0:T(8,128)}, f32[2,256,8]{1,2,0:T(8,128)}, f32[2,768,8]{1,2,0:T(8,128)}, f32[2,256,8]{1,2,0:T(8,128)}, ...) | async-done | bytes 213744 | tf_op jit(solution)/shard_map/psum | solution.py:429
  856.0 39.7 %all-reduce.11.cloned.1.call-done = (f32[256,8]{0,1:T(8,128)}, f32[2,768,8]{1,2,0:T(8,128)}, f32[2,256,8]{1,2,0:T(8,128)}, f32[2,768,8]{1,2,0:T(8,128)}, f32[2,2...) async-done(((f32[256,8]{0,1:T(8,128)}, f32[2,768,8]{1,2,0:T(8,128)}, f32[2,256,8]{1,2,0:T(8,128)}, f32[2,768,8]{1,2,0:T(8,128)}, f32[2,256,8]{1,2,0:T(8,128)}, ...) | async-done | bytes 213744 | tf_op jit(solution)/shard_map/psum | solution.py:432
  (695 shorter events, 334.4 us)
Async XLA Ops:
  7.2 676.8 %copy-start = (f32[2,768,8]{1,2,0:T(8,128)S(1)}, f32[2,768,8]{1,2,0:T(8,128)}, u32[]{:S(2)}) copy-start(f32[2,768,8]{1,2,0:T(8,128)} %param.59) | copy-start | bytes 147460
  7.2 627.2 %reduce-scatter.11.cloned.1.call-start = ((), (), s32[]{:S(2)}) async-start(), calls=%async_computation.8 | async-start | bytes 589824 | tf_op jit(solution)/shard_map/reduce_scatter | solution.py:393
  8.1 199.0 %copy-start.160 = (f32[256]{0:T(256)}, f32[256]{0:T(256)S(1)}, u32[]{:S(2)}) copy-start(f32[256]{0:T(256)S(1)} %get-tuple-element.157) | copy-start | bytes 3076
  8.1 199.0 %copy-start.163 = (f32[256]{0:T(256)}, f32[256]{0:T(256)S(1)}, u32[]{:S(2)}) copy-start(f32[256]{0:T(256)S(1)} %get-tuple-element.158) | copy-start | bytes 3076
  13.3 193.8 %copy-start.167 = (f32[256]{0:T(256)}, f32[256]{0:T(256)S(1)}, u32[]{:S(2)}) copy-start(f32[256]{0:T(256)S(1)} %get-tuple-element.152) | copy-start | bytes 3076
  13.3 197.3 %copy-start.169 = (f32[256]{0:T(256)}, f32[256]{0:T(256)S(1)}, u32[]{:S(2)}) copy-start(f32[256]{0:T(256)S(1)} %get-tuple-element.146) | copy-start | bytes 3076
  23.8 82.9 %copy-start.102 = (s32[1,196,49]{2,1,0:T(8,128)}, s32[1,196,49]{2,1,0:T(8,128)S(1)}, u32[]{:S(2)}) copy-start(s32[1,196,49]{2,1,0:T(8,128)S(1)} %copy.323) | copy-start | bytes 115252
  23.9 76.0 %copy-start.100 = (s32[1,196,49]{2,1,0:T(8,128)}, s32[1,196,49]{2,1,0:T(8,128)S(1)}, u32[]{:S(2)}) copy-start(s32[1,196,49]{2,1,0:T(8,128)S(1)} %copy.322) | copy-start | bytes 115252
  233.6 70.2 %copy-start.17 = (f32[12,196,256]{2,1,0:T(8,128)}, f32[12,196,256]{2,1,0:T(8,128)S(1)}, u32[]{:S(2)}) copy-start(f32[12,196,256]{2,1,0:T(8,128)S(1)} %get-tuple-element.179) | copy-start | bytes 7225348
  483.2 152.3 %reduce-scatter.17.cloned.1.call-start = ((), (), s32[]{:S(2)}) async-start(), calls=%async_computation.11 | async-start | bytes 1179648 | tf_op jit(solution)/shard_map/reduce_scatter | solution.py:397
  484.6 152.1 %reduce-scatter.7.cloned.1.call-start = ((), (), s32[]{:S(2)}) async-start(), calls=%async_computation.6 | async-start | bytes 1327104 | tf_op jit(solution)/shard_map/reduce_scatter | solution.py:396
  563.4 78.9 %reduce-scatter.15.cloned.1.call-start = ((), (), s32[]{:S(2)}) async-start(), calls=%async_computation.10 | async-start | bytes 1769472 | tf_op jit(solution)/shard_map/reduce_scatter | solution.py:395
  569.9 114.1 %reduce-scatter.13.cloned.1.call-start = ((), (), s32[]{:S(2)}) async-start(), calls=%async_computation.9 | async-start | bytes 1769472 | tf_op jit(solution)/shard_map/reduce_scatter | solution.py:394
  578.1 147.6 %reduce-scatter.9.cloned.1.call-start = ((), (), s32[]{:S(2)}) async-start(), calls=%async_computation.7 | async-start | bytes 1769472 | tf_op jit(solution)/shard_map/reduce_scatter | solution.py:392
  593.9 251.4 %all-reduce.9.cloned.1.call-start = ((), (), s32[]{:S(2)}) async-start(), calls=%async_computation.12 | async-start | bytes 434176 | tf_op jit(solution)/shard_map/psum | solution.py:429
  628.5 97.1 %copy-start.50 = (f32[1,2,32,768]{3,2,1,0:T(8,128)S(1)}, f32[1,2,32,768]{3,2,1,0:T(8,128)}, u32[]{:S(2)}) copy-start(f32[1,2,32,768]{3,2,1,0:T(8,128)} %param.51) | copy-start | bytes 589828
  628.6 97.1 %copy-start.162 = (f32[2,768,8]{1,2,0:T(8,128)S(1)}, f32[2,768,8]{1,2,0:T(8,128)}, u32[]{:S(2)}) copy-start(f32[2,768,8]{1,2,0:T(8,128)} %param.57) | copy-start | bytes 147460
  634.4 155.3 %copy-start.83 = (f32[2,32,256]{2,1,0:T(8,128)S(1)}, f32[2,32,256]{2,1,0:T(8,128)}, u32[]{:S(2)}) copy-start(f32[2,32,256]{2,1,0:T(8,128)} %reduce-scatter.11.cloned.1.call-done) | copy-start | bytes 196612
  635.5 155.8 %copy-start.70 = (f32[32,1000]{1,0:T(8,128)S(1)}, f32[32,1000]{1,0:T(8,128)}, u32[]{:S(2)}) copy-start(f32[32,1000]{1,0:T(8,128)} %reduce-scatter.17.cloned.1.call-done) | copy-start | bytes 384004
  636.7 152.2 %copy-start.68 = (f32[144,256]{1,0:T(8,128)S(1)}, f32[144,256]{1,0:T(8,128)}, u32[]{:S(2)}) copy-start(f32[144,256]{1,0:T(8,128)} %reduce-scatter.7.cloned.1.call-done) | copy-start | bytes 442372
  642.4 148.1 %copy-start.55 = (f32[2,96,256]{2,1,0:T(8,128)S(1)}, f32[2,96,256]{2,1,0:T(8,128)}, u32[]{:S(2)}) copy-start(f32[2,96,256]{2,1,0:T(8,128)} %reduce-scatter.15.cloned.1.call-done) | copy-start | bytes 589828
  684.0 109.0 %copy-start.52 = (f32[2,32,768]{2,1,0:T(8,128)S(1)}, f32[2,32,768]{2,1,0:T(8,128)}, u32[]{:S(2)}) copy-start(f32[2,32,768]{2,1,0:T(8,128)} %reduce-scatter.13.cloned.1.call-done) | copy-start | bytes 589828
  725.7 66.5 %copy-start.53 = (f32[2,32,768]{2,1,0:T(8,128)S(1)}, f32[2,32,768]{2,1,0:T(8,128)}, u32[]{:S(2)}) copy-start(f32[2,32,768]{2,1,0:T(8,128)} %reduce-scatter.9.cloned.1.call-done) | copy-start | bytes 589828
  790.5 105.2 %copy-start.114 = (f32[10616]{0:T(1024)S(1)}, f32[10616]{0:T(1024)}, u32[]{:S(2)}) copy-start(f32[10616]{0:T(1024)} %param.62) | copy-start | bytes 127396
  791.3 105.8 %copy-start.113 = (f32[2,32,256]{2,1,0:T(8,128)S(1)}, f32[2,32,256]{2,1,0:T(8,128)}, u32[]{:S(2)}) copy-start(f32[2,32,256]{2,1,0:T(8,128)} %param.40) | copy-start | bytes 196612
  791.3 105.8 %copy-start.155 = (f32[2,32,256]{2,1,0:T(8,128)S(1)}, f32[2,32,256]{2,1,0:T(8,128)}, u32[]{:S(2)}) copy-start(f32[2,32,256]{2,1,0:T(8,128)} %param.46) | copy-start | bytes 196612
  792.1 106.7 %copy-start.88 = (f32[32,1000]{1,0:T(8,128)S(1)}, f32[32,1000]{1,0:T(8,128)}, u32[]{:S(2)}) copy-start(f32[32,1000]{1,0:T(8,128)} %param.43) | copy-start | bytes 384004
  792.1 106.7 %copy-start.146 = (f32[32,1000]{1,0:T(8,128)S(1)}, f32[32,1000]{1,0:T(8,128)}, u32[]{:S(2)}) copy-start(f32[32,1000]{1,0:T(8,128)} %param.49) | copy-start | bytes 384004
  793.0 107.6 %copy-start.85 = (f32[144,256]{1,0:T(8,128)S(1)}, f32[144,256]{1,0:T(8,128)}, u32[]{:S(2)}) copy-start(f32[144,256]{1,0:T(8,128)} %param.38) | copy-start | bytes 442372
  793.0 107.6 %copy-start.145 = (f32[144,256]{1,0:T(8,128)S(1)}, f32[144,256]{1,0:T(8,128)}, u32[]{:S(2)}) copy-start(f32[144,256]{1,0:T(8,128)} %param.44) | copy-start | bytes 442372
  845.3 57.0 %copy-start.119 = (f32[2,32,768]{2,1,0:T(8,128)S(1)}, f32[2,32,768]{2,1,0:T(8,128)}, u32[]{:S(2)}) copy-start(f32[2,32,768]{2,1,0:T(8,128)} %param.45) | copy-start | bytes 589828
  855.2 40.4 %all-reduce.11.cloned.1.call-start = ((), (), s32[]{:S(2)}) async-start(), calls=%async_computation.13 | async-start | bytes 434176 | tf_op jit(solution)/shard_map/psum | solution.py:432
  (184 other events, 1709.2 us)
Sparse Core Ops, SparseCore 0:
  483.3 34.2 reduce-scatter.10
  521.1 36.0 reduce-scatter.16
  563.6 37.0 reduce-scatter.6
  603.8 38.4 reduce-scatter.14
  645.5 38.4 reduce-scatter.12
  687.2 38.4 reduce-scatter.8
  794.0 51.3 all-reduce.8
  859.2 36.3 all-reduce.10
where the time goes:
time: 923 us; the launch traced here: 917 us
  matrix products  264 us (29%)
  blocking collectives  181 us (20%)
  other arithmetic  180 us (20%)
  waiting for transfers between devices  177 us (19%)
  local copies, waits for them, and re-layouts  96.6 us (10%)
  between operations  18.2 us (2%)
    psum x1, waiting for transfers between devices, body(): lax.psum((local_q[0], local_q[1], local_q[2], local_q[3], local_q[4], loc...  51.5 us
    reduce_sum x2, other arithmetic, layer_backward(): g_bias_map = jnp.sum(d_scores.astype(jnp.float32), axis=0)  41.1 us
    reduce_scatter x1, waiting for transfers between devices, body(): lax.psum_scatter(stacks[2], 'fsdp', scatter_dimension=1, tiled=True)  40.4 us
    reduce_scatter x1, waiting for transfers between devices, body(): lax.psum_scatter(stacks[0], 'fsdp', scatter_dimension=1, tiled=True)  40.3 us
    psum x1, blocking collectives, body(): lax.psum((jnp.sum(live_mask * losses), jnp.sum(live_mask)), ('rep', 'fsdp'))  39.9 us
    psum x1, waiting for transfers between devices, body(): lax.psum((q_rows[0], q_rows[1], q_rows[2], q_rows[3], q_rows[4], q_rows[5...  39.7 us
    convert_element_type x2, other arithmetic, layer_forward(): active = jax.nn.gelu(pre_act, approximate=False).astype(jnp.bfloat16)  35.5 us
    slice x1, local copies, waits for them, and re-layouts, patches_of(): blocks[:, row_off // 2:row_off // 2 + GRID, row_off % 2, col_off // 2:col...  32.2 us
  transfers between devices with their start and end apart: 8, of which 5 were waited for; matrix products, arithmetic and copies ran while one was open for 17% of the time, Pallas kernels for 0%

commit v1 on v0

v1 whole, which is shorter than its diff:
```python
import functools
import types

import jax
import jax.numpy as jnp
import numpy as np
from jax import lax
from jax.experimental import pallas as pl
from jax.experimental.pallas import tpu as pltpu
from jax.sharding import PartitionSpec as P

D = 256
HEADS = 8
HEAD = 32
FF = 768
CLASSES = 1000
CPAD = 1024
CIN = 128
GRID = 14
KER = 7
LAYERS = 2
PIX = 196
RB = 169
RANK = 8

EPSILON = 1e-05
MASKED = -1000000000.0
MOMENTUM = 0.9
LEARN_RATE = 16.0
SMALL_RATE = 4.0
PRECISE = lax.Precision.HIGHEST
SCALE = HEAD ** (-0.5)

COLS = 16
TOK = GRID * COLS
KEYS = 128
HALF = 128
PARTS = 3 * CIN
F32 = jnp.float32
BF16 = jnp.bfloat16
VMEM_LIMIT = 58 * 1024 * 1024

GROUPS = (
    ((0, 80, 0), (80, 32, 32), (112, 32, 64), (144, 80, 96)),
    ((0, 112, 0), (112, 112, 96)),
)


def row_order(layer):
    if layer % 2 == 0:
        return list(range(GRID))
    return [*range(0, GRID, 2), *range(1, GRID, 2)]


def window_start(cell, dil):
    residue, position = cell % dil, cell // dil
    length = (GRID - residue + dil - 1) // dil
    return min(max(position - KER // 2, 0), length - KER)


def in_window(query, key, dil):
    if query % dil != key % dil:
        return False
    first = window_start(query, dil)
    return first <= key // dil < first + KER


@functools.lru_cache(None)
def static_maps(layer):
    dil = 1 + layer % 2
    order = row_order(layer)
    rows_hot = np.zeros((GRID * 8, 16), np.float32)
    mask = np.zeros((TOK, KEYS), np.float32)
    for q0, nq, k0 in GROUPS[layer % 2]:
        for place in range(q0 // COLS, (q0 + nq) // COLS):
            qy = order[place]
            for j in range(8):
                ky = order[k0 // COLS + j]
                if not in_window(qy, ky, dil):
                    continue
                rows_hot[place * 8 + j, ky // dil - qy // dil + KER - 1] = 1.0
                for x in range(GRID):
                    for kx in range(GRID):
                        if in_window(x, kx, dil):
                            mask[place * COLS + x, j * COLS + kx] = 1.0
    shifts = np.zeros((COLS, KEYS, KEYS), np.float32)
    for x in range(GRID):
        for kx in range(GRID):
            if in_window(x, kx, dil):
                dx = kx // dil - x // dil + KER - 1
                for j in range(8):
                    shifts[x, j * COLS + dx, j * COLS + kx] = 1.0
    return rows_hot, shifts, mask


def norm_stats(values):
    centred = values - jnp.mean(values, axis=-1, keepdims=True)
    rstd = lax.rsqrt(jnp.mean(centred * centred, axis=-1, keepdims=True) + EPSILON)
    return centred * rstd, rstd


def norm_back(grad, xhat, rstd, gain):
    scaled = grad * gain
    mean_one = jnp.mean(scaled, axis=-1, keepdims=True)
    mean_two = jnp.mean(scaled * xhat, axis=-1, keepdims=True)
    return rstd * (scaled - mean_one - xhat * mean_two)


def col_sum(values):
    return jnp.sum(values, axis=0, keepdims=True)


def dot_nn(a, b, **kw):
    return lax.dot_general(a, b, (((1,), (0,)), ((), ())), preferred_element_type=F32, **kw)


def dot_nt(a, b, **kw):
    return lax.dot_general(a, b, (((1,), (1,)), ((), ())), preferred_element_type=F32, **kw)


def dot_tn(a, b, **kw):
    return lax.dot_general(a, b, (((0,), (0,)), ((), ())), preferred_element_type=F32, **kw)


ERFC_T = 0.44
ERFC_POLY = (
    0.24822096599679971,
    0.24887097779118345,
    0.21731489562842682,
    0.21580753897325447,
    -0.020171305217729862,
    0.2966767736009737,
    -0.2779414931115683,
    0.07122182759012696,
)


def gelu_parts(x):
    bell = jnp.exp(-0.5 * x * x)
    t = 1.0 / (1.0 + (ERFC_T * 0.5**0.5) * jnp.abs(x))
    poly = jnp.full_like(t, 0.5 * ERFC_POLY[-1])
    for c in ERFC_POLY[-2::-1]:
        poly = poly * t + 0.5 * c
    tail = poly * t * bell
    cdf = jnp.where(x < 0, tail, 1.0 - tail)
    return x * cdf, cdf + x * bell * (1.0 / (2.0 * np.pi) ** 0.5)


def head_masks():
    lane = lax.broadcasted_iota(jnp.int32, (1, HALF), 1)
    return [jnp.where(lane // HEAD == h, 1.0, 0.0).astype(BF16) for h in range(4)]


def spread_heads(block, masks):
    return jnp.concatenate([block * m for m in masks], axis=0)


def whole(shape):
    return pl.BlockSpec(shape, lambda *_: (0,) * len(shape))


def params(n=1):
    return pltpu.CompilerParams(
        dimension_semantics=("arbitrary",) * n, vmem_limit_bytes=VMEM_LIMIT
    )


def call(name, kernel, steps, me, ins, outs, scratch):
    names = ["me", *[e[0] for e in ins], *[e[0] for e in outs], *[e[0] for e in scratch]]

    def body(*refs):
        kernel(types.SimpleNamespace(**dict(zip(names, refs, strict=True))))

    results = pl.pallas_call(
        body,
        grid_spec=pltpu.PrefetchScalarGridSpec(
            num_scalar_prefetch=1,
            grid=(steps,),
            in_specs=[e[2] or whole(e[1].shape) for e in ins],
            out_specs=[e[3] or whole(e[1]) for e in outs],
            scratch_shapes=[pltpu.VMEM(e[1], e[2]) for e in scratch],
        ),
        out_shape=[jax.ShapeDtypeStruct(e[1], e[2]) for e in outs],
        compiler_params=params(),
        name=name,
    )(me, *[e[1] for e in ins])
    return types.SimpleNamespace(**dict(zip([e[0] for e in outs], results, strict=True)))


def patch_kernel(feat_ref, out_ref, wide_ref, patch_ref):
    @pl.when(pl.program_id(0) == 0)
    def _():
        patch_ref[...] = jnp.zeros_like(patch_ref)

    wide_ref[:, 0 : 2 * GRID, :] = feat_ref[0].astype(F32)
    even = wide_ref[:, pl.ds(0, GRID, stride=2), :]
    odd = wide_ref[:, pl.ds(1, GRID, stride=2), :]
    patch_ref[:, 1 : GRID + 1, 0:CIN] = odd
    patch_ref[:, 0:GRID, CIN : 2 * CIN] = even
    patch_ref[:, 0:GRID, 2 * CIN : 3 * CIN] = odd
    both = patch_ref[...].astype(BF16).reshape(GRID, 2, COLS, PARTS)
    for par in range(2):
        out_ref[0, par] = both[:, par].reshape(TOK, PARTS)


def make_patches(features):
    slots = features.shape[0]
    return pl.pallas_call(
        patch_kernel,
        grid=(slots,),
        in_specs=[pl.BlockSpec((1, 2 * GRID, 2 * GRID, CIN), lambda i: (i, 0, 0, 0))],
        out_specs=pl.BlockSpec((1, 2, TOK, PARTS), lambda i: (i, 0, 0, 0)),
        out_shape=jax.ShapeDtypeStruct((slots, 2, TOK, PARTS), BF16),
        scratch_shapes=[
            pltpu.VMEM((2 * GRID, 32, CIN), F32),
            pltpu.VMEM((2 * GRID, COLS, PARTS), F32),
        ],
        compiler_params=params(),
        name="patches",
    )(features)


def bias_kernel(rows_ref, shift_ref, mask_ref, out_ref, flat_ref):
    def at_column(x, _):
        part = dot_nn(rows_ref[0], shift_ref[0, x], precision=PRECISE)
        flat_ref[pl.ds(x, HEADS * GRID, stride=COLS), :] = part
        return 0

    lax.fori_loop(0, COLS, at_column, 0)
    for h in range(HEADS):
        block = flat_ref[h * TOK : (h + 1) * TOK, :]
        out_ref[0, h] = jnp.where(mask_ref[0] > 0.5, block, MASKED)


def make_bias(tables):
    maps = [static_maps(layer) for layer in range(LAYERS)]
    padded = jnp.pad(tables, ((0, 0), (0, 0), (0, 3), (0, 3)))
    hots = jnp.asarray(np.stack([m[0] for m in maps]))
    rows = jnp.einsum("lpd,lhde->lhpe", hots, padded, precision=PRECISE)
    rows = rows.reshape(LAYERS, HEADS * GRID, KEYS)
    shifts = jnp.asarray(np.stack([m[1] for m in maps]))
    masks = jnp.asarray(np.stack([m[2] for m in maps]))
    return pl.pallas_call(
        bias_kernel,
        grid=(LAYERS,),
        in_specs=[
            pl.BlockSpec((1, HEADS * GRID, KEYS), lambda i: (i, 0, 0)),
            pl.BlockSpec((1, COLS, KEYS, KEYS), lambda i: (i, 0, 0, 0)),
            pl.BlockSpec((1, TOK, KEYS), lambda i: (i, 0, 0)),
        ],
        out_specs=pl.BlockSpec((1, HEADS, TOK, KEYS), lambda i: (i, 0, 0, 0)),
        out_shape=jax.ShapeDtypeStruct((LAYERS, HEADS, TOK, KEYS), F32),
        scratch_shapes=[pltpu.VMEM((HEADS * TOK, KEYS), F32)],
        compiler_params=params(),
        name="bias",
    )(rows, shifts, masks)


def table_grad_kernel(grad_ref, shift_ref, out_ref):
    def at_column(x, total):
        part = grad_ref[0, pl.ds(x, HEADS * GRID, stride=COLS), :]
        return total + dot_nt(part, shift_ref[0, x], precision=PRECISE)

    out_ref[0] = lax.fori_loop(0, COLS, at_column, jnp.zeros((HEADS * GRID, KEYS), F32))


def table_grad(bias_grad, layer):
    rows_hot, shifts, _ = static_maps(layer)
    rows = pl.pallas_call(
        table_grad_kernel,
        grid=(1,),
        in_specs=[whole((1, HEADS * TOK, KEYS)), whole((1, COLS, KEYS, KEYS))],
        out_specs=whole((1, HEADS * GRID, KEYS)),
        out_shape=jax.ShapeDtypeStruct((1, HEADS * GRID, KEYS), F32),
        compiler_params=params(),
        name="table_grad",
    )(bias_grad.reshape(1, HEADS * TOK, KEYS), jnp.asarray(shifts)[None])
    out = jnp.einsum(
        "pd,hpe->hde", jnp.asarray(rows_hot), rows.reshape(HEADS, GRID * 8, 16), precision=PRECISE
    )
    return out[:, : 2 * KER - 1, : 2 * KER - 1]


def pieces_of(shards, group):
    narrow, wide = D // shards, FF // shards
    sizes = [("qkv", narrow, 3), ("proj", narrow, 1), ("up", narrow, 3), ("down", wide, 1)]
    if group == 0:
        sizes = [("conv", 9 * CIN // shards, 1)] + sizes
    else:
        sizes = sizes + [("head", narrow, 4)]
    out, at = {}, 0
    for name, rows, blocks in sizes:
        out[name] = (at, rows, blocks)
        at += rows * blocks
    return out, at


def pack(parts):
    out = []
    for part in parts:
        if part.shape[1] == CLASSES:
            part = jnp.pad(part, ((0, 0), (0, CPAD - CLASSES)))
        out += [part[:, c : c + D] for c in range(0, part.shape[1], D)]
    return jnp.concatenate(out, axis=0)


SPLIT = (240, 224)
SHARDS = 8


def unpack_weights(me, sources, targets, group):
    layout, _ = pieces_of(SHARDS, group)
    for ref, low, high, offsets in sources:
        for p, offset in enumerate(offsets):
            owner = me ^ offset
            for name, target in targets.items():
                at, rows, blocks = layout[name]
                if not low <= at < high:
                    continue
                place = pl.ds(pl.multiple_of(owner * rows, 16), rows)
                for c in range(blocks):
                    first = at - low + c * rows
                    target[place, c * D : (c + 1) * D] = ref[p, first : first + rows, :]


def attend(layer, item, joined_ref, bias_ref, probs_ref, mixed_ref):
    masks = head_masks()
    base = item * TOK
    for q0, nq, k0 in GROUPS[layer]:
        for hf in range(2):
            lanes = slice(hf * HALF, (hf + 1) * HALF)
            at = lambda which: slice(which * D + hf * HALF, which * D + (hf + 1) * HALF)
            query = joined_ref[base + q0 : base + q0 + nq, at(0)]
            keys = spread_heads(joined_ref[base + k0 : base + k0 + KEYS, at(1)], masks)
            values = spread_heads(joined_ref[base + k0 : base + k0 + KEYS, at(2)], masks)
            scores = dot_nt(query, keys)
            low = []
            for h in range(4):
                head = hf * 4 + h
                s = scores[:, h * KEYS : (h + 1) * KEYS] * SCALE + bias_ref[0, head, q0 : q0 + nq, :]
                e = jnp.exp(s - jnp.max(s, axis=-1, keepdims=True))
                p = e * (1.0 / jnp.sum(e, axis=-1, keepdims=True))
                probs_ref[item, q0 : q0 + nq, head * KEYS : (head + 1) * KEYS] = p
                low.append(p.astype(BF16))
            mixed = dot_nn(jnp.concatenate(low, axis=1), values)
            mixed_ref[base + q0 : base + q0 + nq, lanes] = mixed.astype(BF16)


def layer_forward(layer, hidden, vec_ref, weights, bias_ref, outs, items):
    joined_ref, probs_ref, mixed_ref, after_ref, slope_ref, active_ref = outs
    vec = lambda i: vec_ref[i : i + 1, :]
    xhat, _ = norm_stats(hidden)
    normed = (xhat * vec(0) + vec(1)).astype(BF16)
    for c in range(3):
        part = dot_nn(normed, weights["qkv"][:, c * D : (c + 1) * D])
        if c != 1:
            part = part + vec(2 if c == 0 else 3)
        joined_ref[:, c * D : (c + 1) * D] = part.astype(BF16)
    for item in range(items):
        attend(layer, item, joined_ref, bias_ref, probs_ref, mixed_ref)
    after = hidden + (dot_nn(mixed_ref[...], weights["proj"][...]) + vec(4))
    after_ref[...] = after
    xhat, _ = norm_stats(after)
    normed = (xhat * vec(5) + vec(6)).astype(BF16)
    total = None
    for c in range(3):
        pre = dot_nn(normed, weights["up"][:, c * D : (c + 1) * D]) + vec(8 + c)
        active, slope = gelu_parts(pre)
        active = active.astype(BF16)
        slope_ref[:, c * D : (c + 1) * D] = slope
        active_ref[:, c * D : (c + 1) * D] = active
        part = dot_nn(active, weights["down"][c * D : (c + 1) * D, :])
        total = part if total is None else total + part
    return after + (total + vec(7))


def conv_taps(patch_ref, item):
    odd = patch_ref[item, 1]
    up = jnp.concatenate([jnp.zeros((COLS, PARTS), BF16), odd[: TOK - COLS]], axis=0)
    return up, patch_ref[item, 0], odd


CACHE = (
    ("joined", 3 * D, BF16),
    ("probs", None, F32),
    ("mixed", D, BF16),
    ("after", D, F32),
    ("slope", FF, F32),
    ("active", FF, BF16),
)
MATRICES = (("qkv", (D, FF)), ("proj", (D, D)), ("up", (D, FF)), ("down", (FF, D)))
MATRIX_NAMES = [m[0] for m in MATRICES]


def token_spec(items, width=D):
    return pl.BlockSpec((items * TOK, width), lambda i, *_: (i, 0))


def cache_entries(slots, items):
    out = []
    for name, width, dtype in CACHE:
        if width is None:
            spec = pl.BlockSpec((items, TOK, HEADS * KEYS), lambda i, *_: (i, 0, 0))
            out.append((name, (slots, TOK, HEADS * KEYS), dtype, spec))
        else:
            out.append((name, (slots * TOK, width), dtype, token_spec(items, width)))
    return out


def caches_of(r):
    return tuple(getattr(r, entry[0]) for entry in CACHE)


def bias_spec(layer):
    return pl.BlockSpec((1, HEADS, TOK, KEYS), lambda i, *_: (layer, 0, 0, 0))


def patch_spec(items):
    return pl.BlockSpec((items, 2, TOK, PARTS), lambda i, *_: (i, 0, 0, 0))


def source_entries(sources):
    return [(f"source{i}", array, None) for i, (array, *_) in enumerate(sources)]


def sources_of(r, sources):
    return [(getattr(r, f"source{i}"), *entry[1:]) for i, entry in enumerate(sources)]


def forward_zero(me, patches, sources, vec, conv_vec, bias, items):
    slots = patches.shape[0]

    def kernel(r):
        names = ["conv_w", *MATRIX_NAMES]
        weights = {n: getattr(r, n) for n in names}

        @pl.when(pl.program_id(0) == 0)
        def _():
            targets = {n.removesuffix("_w"): ref for n, ref in weights.items()}
            unpack_weights(r.me[0], sources_of(r, sources), targets, 0)

        for item in range(items):
            taps = conv_taps(r.patch, item)
            total = None
            for a in range(3):
                part = dot_nn(taps[a], r.conv_w[a * PARTS : (a + 1) * PARTS, :])
                total = part if total is None else total + part
            r.conv[item * TOK : (item + 1) * TOK, :] = total + r.conv_vec[0:1, :]
        xhat, _ = norm_stats(r.conv[...])
        hidden = xhat * r.conv_vec[1:2, :] + r.conv_vec[2:3, :]
        hidden = layer_forward(0, hidden, r.vec, weights, r.bias, caches_of(r), items)
        for item in range(items):
            for place, row in enumerate(row_order(1)):
                r.hidden[item * TOK + place * COLS : item * TOK + (place + 1) * COLS, :] = hidden[
                    item * TOK + row * COLS : item * TOK + (row + 1) * COLS
                ]

    return call(
        "forward_zero",
        kernel,
        slots // items,
        me,
        [
            ("patch", patches, patch_spec(items)),
            *source_entries(sources),
            ("vec", vec, None),
            ("conv_vec", conv_vec, None),
            ("bias", bias, bias_spec(0)),
        ],
        [
            ("hidden", (slots * TOK, D), F32, token_spec(items)),
            ("conv", (slots * TOK, D), F32, token_spec(items)),
            *cache_entries(slots, items),
            *[(n, shape, BF16, None) for n, shape in MATRICES],
        ],
        [("conv_w", (9 * CIN, D), BF16)],
    )


def real_cells():
    place = lax.broadcasted_iota(jnp.int32, (TOK, 1), 0)
    return jnp.where(place % COLS < GRID, 1.0, 0.0)


def classify(r):
    pooled = r.pooled[...].astype(BF16)
    logits = dot_nn(pooled, r.head[...]) + r.head_bias[...]
    peak = jnp.max(logits, axis=-1, keepdims=True)
    log_total = peak + jnp.log(jnp.sum(jnp.exp(logits - peak), axis=-1, keepdims=True))
    lane = lax.broadcasted_iota(jnp.int32, logits.shape, 1)
    onehot = jnp.where(r.label[:, 0:1] == lane, 1.0, 0.0)
    picked = jnp.sum(onehot * logits, axis=-1, keepdims=True)
    live = r.live[:, 0:1]
    r.loss[...] = jnp.broadcast_to(col_sum(live * (log_total - picked)), r.loss.shape)
    d_logits = (jnp.exp(logits - log_total) - onehot) * (r.inverse[:, 0:1] * live)
    d_logits = jnp.where(lane < CLASSES, d_logits, 0.0).astype(BF16)
    r.head_grad[...] = dot_tn(pooled, d_logits)
    r.head_bias_grad[...] = col_sum(d_logits.astype(F32))
    r.d_pooled[...] = dot_nt(d_logits, r.head[...]) * (1.0 / PIX)


def forward_one(me, hidden, sources, vec, final, bias, head_bias, label, live, inverse, items):
    slots = hidden.shape[0] // TOK
    rows = label.shape[0]

    def kernel(r):
        weights = {n: getattr(r, n) for n in MATRIX_NAMES}
        step = pl.program_id(0)

        @pl.when(step == 0)
        def _():
            unpack_weights(r.me[0], sources_of(r, sources), weights | dict(head=r.head), 1)
            r.pooled[...] = jnp.zeros_like(r.pooled)

        out = layer_forward(1, r.hidden[...], r.vec, weights, r.bias, caches_of(r), items)
        r.out[...] = out
        xhat, _ = norm_stats(out)
        normed = xhat * r.final[0:1, :] + r.final[1:2, :]
        real = real_cells()
        for item in range(items):
            mean = col_sum(normed[item * TOK : (item + 1) * TOK] * real) * (1.0 / PIX)
            r.pooled[pl.ds(step * items + item, 1), :] = mean

        @pl.when(step == pl.num_programs(0) - 1)
        def _():
            classify(r)

    return call(
        "forward_one",
        kernel,
        slots // items,
        me,
        [
            ("hidden", hidden, token_spec(items)),
            *source_entries(sources),
            ("vec", vec, None),
            ("final", final, None),
            ("bias", bias, bias_spec(1)),
            ("head_bias", head_bias, None),
            ("label", label, None),
            ("live", live, None),
            ("inverse", inverse, None),
        ],
        [
            ("out", (slots * TOK, D), F32, token_spec(items)),
            *cache_entries(slots, items),
            *[(n, shape, BF16, None) for n, shape in MATRICES],
            ("loss", (8, 128), F32, None),
            ("head_grad", (D, CPAD), F32, None),
            ("head_bias_grad", (1, CPAD), F32, None),
            ("d_pooled", (rows, D), F32, None),
        ],
        [("head", (D, CPAD), BF16), ("pooled", (rows, D), F32)],
    )


def attend_back(layer, item, first, joined_ref, probs_ref, dmix_ref, djoin_ref, dkv_ref, bgrad_ref):
    masks = head_masks()
    base = item * TOK
    dkv_ref[...] = jnp.zeros_like(dkv_ref)
    for q0, nq, k0 in GROUPS[layer]:
        qrows = slice(base + q0, base + q0 + nq)
        krows = slice(base + k0, base + k0 + KEYS)
        for hf in range(2):
            lanes = slice(hf * HALF, (hf + 1) * HALF)
            at = lambda which: slice(which * D + hf * HALF, which * D + (hf + 1) * HALF)
            query = spread_heads(joined_ref[qrows, at(0)], masks)
            keys = spread_heads(joined_ref[krows, at(1)], masks)
            values = spread_heads(joined_ref[krows, at(2)], masks)
            d_mix = dmix_ref[qrows, lanes]
            d_probs = dot_nt(d_mix, values)
            d_low, p_low = [], []
            for h in range(4):
                head = hf * 4 + h
                p = probs_ref[item, q0 : q0 + nq, head * KEYS : (head + 1) * KEYS]
                dp = d_probs[:, h * KEYS : (h + 1) * KEYS]
                ds = (p * (dp - jnp.sum(dp * p, axis=-1, keepdims=True))).astype(BF16)
                place = slice(head * TOK + q0, head * TOK + q0 + nq)
                bgrad_ref[place, :] += ds.astype(F32)
                d_low.append(ds)
                p_low.append(p.astype(BF16))
            d_query = dot_nn(jnp.concatenate(d_low, axis=1), keys) * SCALE
            djoin_ref[qrows, at(0)] = d_query.astype(BF16)
            d_keys = dot_tn(jnp.concatenate(d_low, axis=0), query)
            d_values = dot_tn(jnp.concatenate(p_low, axis=0), spread_heads(d_mix, masks))
            dkv_ref[k0 : k0 + KEYS, lanes] += d_keys
            dkv_ref[k0 : k0 + KEYS, D + hf * HALF : D + (hf + 1) * HALF] += d_values
    djoin_ref[base : base + TOK, D : 2 * D] = (dkv_ref[:, 0:D] * SCALE).astype(BF16)
    djoin_ref[base : base + TOK, 2 * D : 3 * D] = dkv_ref[:, D : 2 * D].astype(BF16)


def layer_backward(layer, d_out, hidden, vec_ref, weights, caches, work, grads, vgrad_ref, bgrad_ref, items):
    joined_ref, probs_ref, mixed_ref, after_ref, slope_ref, active_ref = caches
    dmix_ref, djoin_ref, dkv_ref = work
    vec = lambda i: vec_ref[i : i + 1, :]

    def add(row, value):
        vgrad_ref[row : row + 1, :] += value

    d_branch = d_out.astype(BF16)
    add(7, col_sum(d_branch.astype(F32)))
    xhat, rstd = norm_stats(after_ref[...])
    normed = (xhat * vec(5) + vec(6)).astype(BF16)
    d_normed = None
    for c in range(3):
        cols = slice(c * D, (c + 1) * D)
        grads["down"][:, cols] += dot_tn(d_branch, active_ref[:, cols])
        d_active = dot_nt(d_branch, weights["down"][cols, :])
        d_pre = (d_active * slope_ref[:, cols]).astype(BF16)
        add(8 + c, col_sum(d_pre.astype(F32)))
        grads["up"][:, cols] += dot_tn(normed, d_pre)
        part = dot_nt(d_pre, weights["up"][:, cols])
        d_normed = part if d_normed is None else d_normed + part
    add(5, col_sum(d_normed * xhat))
    add(6, col_sum(d_normed))
    d_after = d_out + norm_back(d_normed, xhat, rstd, vec(5))
    d_proj = d_after.astype(BF16)
    add(4, col_sum(d_proj.astype(F32)))
    grads["proj"][...] += dot_tn(mixed_ref[...], d_proj)
    dmix_ref[...] = dot_nt(d_proj, weights["proj"][...]).astype(BF16)
    for item in range(items):
        attend_back(layer, item, item == 0, joined_ref, probs_ref, dmix_ref, djoin_ref, dkv_ref, bgrad_ref)
    add(2, col_sum(djoin_ref[:, 0:D].astype(F32)))
    add(3, col_sum(djoin_ref[:, 2 * D : 3 * D].astype(F32)))
    xhat, rstd = norm_stats(hidden)
    normed = (xhat * vec(0) + vec(1)).astype(BF16)
    d_normed = None
    for c in range(3):
        cols = slice(c * D, (c + 1) * D)
        grads["qkv"][:, cols] += dot_tn(normed, djoin_ref[:, cols])
        part = dot_nt(djoin_ref[:, cols], weights["qkv"][:, cols])
        d_normed = part if d_normed is None else d_normed + part
    add(0, col_sum(d_normed * xhat))
    add(1, col_sum(d_normed))
    return d_after + norm_back(d_normed, xhat, rstd, vec(0))


def split_two(x):
    high = x.astype(BF16)
    return high, (x - high.astype(F32)).astype(BF16)


def stack_three(x):
    high = x.astype(BF16).astype(F32)
    mid = (x - high).astype(BF16).astype(F32)
    return jnp.concatenate([high, mid, x - high - mid], axis=0).astype(BF16)


def wide_dot(dot, rows, matrix):
    stacked = stack_three(rows)
    high, low = split_two(matrix)
    out = dot(stacked, high) + dot(stacked, low)
    return out[0:RANK] + out[RANK : 2 * RANK] + out[2 * RANK : 3 * RANK]


def block_of(whole_ref, entry, c):
    at, rows, _ = entry
    return jnp.concatenate(
        [whole_ref[s, at + c * rows : at + (c + 1) * rows, :] for s in range(SHARDS)], axis=0
    )


def finish_grads(r, group, grads):
    layout, _ = pieces_of(SHARDS, group)
    me = r.me[0]
    for name, (at, rows, blocks) in layout.items():
        matrix = grads[name]
        if name in ("down", "conv"):
            matrix = jnp.transpose(matrix[...])
        for s in range(SHARDS):
            for c in range(blocks):
                piece = matrix[s * rows : (s + 1) * rows, c * D : (c + 1) * D]
                r.whole[s, at + c * rows : at + (c + 1) * rows, :] = piece
    r.whole[me] += r.err[...]
    r.own[...] = r.whole[me]
    for j in range(1, SHARDS):
        getattr(r, f"sent{j}")[...] = r.whole[me ^ j].astype(BF16)
    at_lane, at_col = 0, 0
    for name, entry in layout.items():
        total = None
        for c in range(entry[2]):
            part = wide_dot(dot_nt, r.fac[:, at_col : at_col + D], block_of(r.whole, entry, c))
            total = part if total is None else total + part
            at_col += D
        lanes = entry[1] * SHARDS
        r.left[:, at_lane : at_lane + lanes] = total
        at_lane += lanes


def left_lanes(group):
    return sum(rows * SHARDS for _, rows, _ in pieces_of(SHARDS, group)[0].values())


def right_lanes(group):
    return sum(blocks * D for _, _, blocks in pieces_of(SHARDS, group)[0].values())


def backward_outs(group):
    rows = pieces_of(SHARDS, group)[1]
    return [
        ("vgrad", (16, D), F32, None),
        ("bgrad", (HEADS * TOK, KEYS), F32, None),
        ("whole", (SHARDS, rows, D), F32, None),
        ("own", (rows, D), F32, None),
        *[(f"sent{j}", (rows, D), BF16, None) for j in range(1, SHARDS)],
        ("left", (RANK, left_lanes(group)), F32, None),
    ]


def backward_scratch(items):
    return [
        ("d_mixed", (items * TOK, D), BF16),
        ("d_joined", (items * TOK, 3 * D), BF16),
        ("d_keys", (TOK, 2 * D), F32),
        ("g_qkv", (D, FF), F32),
        ("g_proj", (D, D), F32),
        ("g_up", (D, FF), F32),
        ("g_down", (D, FF), F32),
    ]


def start_backward(r, grads):
    r.vgrad[...] = jnp.zeros_like(r.vgrad)
    r.bgrad[...] = jnp.zeros_like(r.bgrad)
    for ref in grads.values():
        ref[...] = jnp.zeros_like(ref)


def cache_inputs(caches, slots, items):
    return [(e[0], getattr(caches, e[0]), e[3]) for e in cache_entries(slots, items)]


def matrix_inputs(caches):
    return [(n, getattr(caches, n), None) for n in MATRIX_NAMES]


def backward_one(me, hidden, forward, vec, final, err, fac, items):
    slots = hidden.shape[0] // TOK

    def kernel(r):
        weights = {n: getattr(r, n) for n in MATRIX_NAMES}
        grads = {n: getattr(r, "g_" + n) for n in MATRIX_NAMES}
        step = pl.program_id(0)

        @pl.when(step == 0)
        def _():
            start_backward(r, grads)

        real = real_cells()
        d_final = jnp.concatenate(
            [real * r.d_pooled[pl.ds(step * items + item, 1), :] for item in range(items)], axis=0
        )
        xhat, rstd = norm_stats(r.out[...])
        r.vgrad[11:12, :] += col_sum(d_final * xhat)
        r.vgrad[12:13, :] += col_sum(d_final)
        d_out = norm_back(d_final, xhat, rstd, r.final[0:1, :])
        work = (r.d_mixed, r.d_joined, r.d_keys)
        r.d_hidden[...] = layer_backward(
            1, d_out, r.hidden[...], r.vec, weights, caches_of(r), work, grads, r.vgrad, r.bgrad, items
        )

        @pl.when(step == pl.num_programs(0) - 1)
        def _():
            finish_grads(r, 1, grads | dict(head=r.head_grad))

    return call(
        "backward_one",
        kernel,
        slots // items,
        me,
        [
            ("out", forward.out, token_spec(items)),
            ("d_pooled", forward.d_pooled, None),
            ("hidden", hidden, token_spec(items)),
            *matrix_inputs(forward),
            ("vec", vec, None),
            ("final", final, None),
            *cache_inputs(forward, slots, items),
            ("head_grad", forward.head_grad, None),
            ("err", err, None),
            ("fac", fac, None),
        ],
        [("d_hidden", hidden.shape, F32, token_spec(items)), *backward_outs(1)],
        backward_scratch(items),
    )


def backward_zero(me, d_hidden, forward, patches, vec, conv_vec, err, fac, items):
    slots = patches.shape[0]

    def kernel(r):
        weights = {n: getattr(r, n) for n in MATRIX_NAMES}
        grads = {n: getattr(r, "g_" + n) for n in [*MATRIX_NAMES, "conv"]}
        step = pl.program_id(0)

        @pl.when(step == 0)
        def _():
            start_backward(r, grads)

        order = row_order(1)
        rows = []
        for item in range(items):
            for row in range(GRID):
                first = item * TOK + order.index(row) * COLS
                rows.append(r.d_hidden[first : first + COLS, :])
        d_out = jnp.concatenate(rows, axis=0)
        conv_hat, conv_rstd = norm_stats(r.conv[...])
        gain = r.conv_vec[1:2, :]
        hidden = conv_hat * gain + r.conv_vec[2:3, :]
        work = (r.d_mixed, r.d_joined, r.d_keys)
        d_conv = layer_backward(
            0, d_out, hidden, r.vec, weights, caches_of(r), work, grads, r.vgrad, r.bgrad, items
        )
        r.vgrad[12:13, :] += col_sum(d_conv * conv_hat)
        r.vgrad[13:14, :] += col_sum(d_conv)
        d_conv = norm_back(d_conv, conv_hat, conv_rstd, gain).astype(BF16)
        r.vgrad[11:12, :] += col_sum(d_conv.astype(F32))
        for item in range(items):
            taps = conv_taps(r.patch, item)
            part = d_conv[item * TOK : (item + 1) * TOK]
            for a in range(3):
                grads["conv"][:, a * PARTS : (a + 1) * PARTS] += dot_tn(part, taps[a])

        @pl.when(step == pl.num_programs(0) - 1)
        def _():
            finish_grads(r, 0, grads)

    return call(
        "backward_zero",
        kernel,
        slots // items,
        me,
        [
            ("d_hidden", d_hidden, token_spec(items)),
            ("conv", forward.conv, token_spec(items)),
            ("patch", patches, patch_spec(items)),
            *matrix_inputs(forward),
            ("vec", vec, None),
            ("conv_vec", conv_vec, None),
            *cache_inputs(forward, slots, items),
            ("err", err, None),
            ("fac", fac, None),
        ],
        backward_outs(0),
        [*backward_scratch(items), ("g_conv", (D, 9 * CIN), F32)],
    )


def inverse_cholesky(gram):
    row = lax.broadcasted_iota(jnp.int32, (1, RANK, 2 * RANK), 1)
    lane = lax.broadcasted_iota(jnp.int32, (1, RANK, 2 * RANK), 2)
    eye = jnp.broadcast_to(jnp.where(lane == row + RANK, 1.0, 0.0), (gram.shape[0], RANK, 2 * RANK))
    work = jnp.concatenate([gram, jnp.zeros_like(gram)], axis=2) + eye
    for k in range(RANK):
        scale = 1.0 / jnp.sqrt(work[:, k : k + 1, k : k + 1])
        pivot = work[:, k : k + 1, :] * scale
        column = work[:, :, k : k + 1] * scale
        work = jnp.where(row > k, work - column * pivot, jnp.where(row == k, pivot, work))
    return work[:, :, RANK : 2 * RANK]


def basis_lanes(group):
    return sum(rows for _, rows, _ in pieces_of(SHARDS, group)[0].values())


def right_factors(me, left, whole_zero, whole_one):
    def kernel(r):
        groups = (r.whole0, r.whole1)
        entries, at = [], 0
        for group in range(2):
            for entry in pieces_of(SHARDS, group)[0].values():
                entries.append((group, entry, at))
                at += entry[1] * SHARDS
        lefts = [r.left[:, at : at + entry[1] * SHARDS] for _, entry, at in entries]
        grams = jnp.stack([dot_nt(x, x, precision=PRECISE) for x in lefts])
        inverses = inverse_cholesky(grams)
        at_col = 0
        rows_of = [[], []]
        for i, (group, entry, _) in enumerate(entries):
            basis = dot_nn(inverses[i], lefts[i], precision=PRECISE)
            rows_of[group].append((basis, entry[1]))
            for c in range(entry[2]):
                r.right[:, at_col : at_col + D] = wide_dot(dot_nn, basis, block_of(groups[group], entry, c))
                at_col += D
        for group, out in ((0, r.basis0), (1, r.basis1)):
            for s in range(SHARDS):
                at = 0
                for basis, rows in rows_of[group]:
                    out[s, :, at : at + rows] = basis[:, s * rows : (s + 1) * rows]
                    at += rows

    return call(
        "right_factors",
        kernel,
        1,
        me,
        [("left", left, None), ("whole0", whole_zero, None), ("whole1", whole_one, None)],
        [
            ("right", (RANK, right_lanes(0) + right_lanes(1)), F32, None),
            ("basis0", (SHARDS, RANK, basis_lanes(0)), F32, None),
            ("basis1", (SHARDS, RANK, basis_lanes(1)), F32, None),
        ],
        [],
    )


def six_products(x, other):
    high = x.astype(BF16).astype(F32)
    mid = (x - high).astype(BF16).astype(F32)
    low = x - high - mid
    terms = [high, mid, high, mid, low, high] if other else [high, high, mid, mid, high, low]
    return jnp.concatenate(terms, axis=0).astype(BF16)


UPDATED = (("conv", 0), ("qkv", 1), ("proj", 1), ("up", 1), ("down", 1), ("head", 0))


def apply_update(me, weights, moms, right_mine, right_all, factors, own, received):
    def kernel(r):
        at_col = 0
        for group in range(2):
            total = getattr(r, f"own{group}")[...]
            for i in range(len(received[group])):
                total = total + getattr(r, f"got{group}_{i}")[...].astype(F32)
            basis = getattr(r, f"basis{group}")
            at_row = 0
            for name, (at, rows, blocks) in pieces_of(SHARDS, group)[0].items():
                left = six_products(basis[0, :, at_row : at_row + rows], False)
                at_row += rows
                whole_matrix = name in ("conv", "head")
                for c in range(blocks):
                    width = min(D, (CLASSES if name == "head" else blocks * D) - c * D)
                    cols = slice(c * D, c * D + width)
                    place = (slice(None), cols) if whole_matrix else (group, slice(None), cols)
                    err_place = (0, slice(None), cols) if whole_matrix else (0, group, slice(None), cols)
                    right = slice(at_col, at_col + D)
                    at_col += D
                    mine = dot_tn(left, six_products(r.right_mine[:, right], True))
                    every = dot_tn(left, six_products(r.right_all[:, right], True))
                    merged = total[at + c * rows : at + (c + 1) * rows]
                    getattr(r, "err_" + name)[err_place] = (merged - mine)[:, :width]
                    mom = MOMENTUM * getattr(r, "mom_" + name)[place] + every[:, :width]
                    getattr(r, "new_mom_" + name)[place] = mom
                    getattr(r, "new_" + name)[place] = getattr(r, "w_" + name)[place] - LEARN_RATE * mom

    names = [n for n, _ in UPDATED]
    mine_spec = lambda x: pl.BlockSpec((1,) + x.shape[1:], lambda i, m: (m[0], 0, 0))
    err_shape = lambda w: (1,) + w.shape
    return call(
        "apply_update",
        kernel,
        1,
        me,
        [
            *[("w_" + n, w, None) for n, w in zip(names, weights)],
            *[("mom_" + n, m, None) for n, m in zip(names, moms)],
            ("right_mine", right_mine, None),
            ("right_all", right_all, None),
            ("basis0", factors[0], mine_spec(factors[0])),
            ("basis1", factors[1], mine_spec(factors[1])),
            ("own0", own[0], None),
            ("own1", own[1], None),
            *[(f"got{g}_{i}", x, None) for g in range(2) for i, x in enumerate(received[g])],
        ],
        [
            *[("new_" + n, w.shape, F32, None) for n, w in zip(names, weights)],
            *[("new_mom_" + n, w.shape, F32, None) for n, w in zip(names, weights)],
            *[("err_" + n, err_shape(w), F32, None) for n, w in zip(names, weights)],
        ],
        [],
    )


def swap(x, offset):
    return lax.ppermute(x, "fsdp", [(i, i ^ offset) for i in range(SHARDS)])


def swap_by_core(x, even, odd):
    return lax.ppermute(x, "fsdp", [(i, i ^ (odd if i & 1 else even)) for i in range(SHARDS)])


def swap_rep(x, offset, reps):
    return lax.ppermute(x, "rep", [(i, i ^ offset) for i in range(reps)])


def gather_halves(first, second, cut, end):
    out = []
    for part, low, high, order in ((first, 0, cut, (4, 2)), (second, cut, end, (2, 4))):
        near = part[None]
        offsets = [0]
        for bit in order:
            near = jnp.concatenate([near, swap(near, bit)], axis=0)
            offsets = offsets + [o ^ bit for o in offsets]
        out.append((near, low, high, tuple(offsets)))
        out.append((swap(near, 1), low, high, tuple(o ^ 1 for o in offsets)))
    return out


def gather_direct(packed):
    end = packed.shape[0]
    out = [(packed[None], 0, end, (0,))]
    for j in range(1, SHARDS):
        out.append((swap(packed, j)[None], 0, end, (j,)))
    return out


def halves(x):
    half = x.shape[1] // 2
    core = lax.axis_index("fsdp") & 1
    first, second = x[:, :half], x[:, half:]
    return jnp.where(core == 0, first, second), jnp.where(core == 0, second, first)


def join_halves(mine, other):
    core = lax.axis_index("fsdp") & 1
    low, high = jnp.where(core == 0, mine, other), jnp.where(core == 0, other, mine)
    return jnp.concatenate([low, high], axis=-1)


def sum_replica(x):
    mine, other = halves(x)
    mine = mine + swap(other, 1)
    mine = mine + swap_by_core(mine, 2, 4)
    return mine + swap_by_core(mine, 4, 2)


def sum_replicas(x, reps):
    bit = 1
    while bit < reps:
        x = x + swap_rep(x, bit, reps)
        bit *= 2
    return x


def pad_lanes(x, lanes):
    return jnp.pad(x, ((0, 0), (0, lanes - x.shape[1])))


def table_at(layer):
    return 3 * D + layer * (11 * D + HEADS * RB)


def small_blocks(small):
    layer_vecs, tables = [], []
    for layer in range(LAYERS):
        at = table_at(layer)
        layer_vecs.append(small[at : at + 11 * D].reshape(11, D))
        tables.append(small[at + 11 * D : at + 11 * D + HEADS * RB])
    at = table_at(LAYERS)
    final = small[at : at + 2 * D].reshape(2, D)
    head_bias = jnp.pad(small[at + 2 * D :][None], ((0, 0), (0, CPAD - CLASSES)), constant_values=-1e30)
    tables = jnp.stack(tables).reshape(LAYERS, HEADS, 2 * KER - 1, 2 * KER - 1)
    return small[: 3 * D].reshape(3, D), layer_vecs, final, tables, head_bias


def small_vector(vgrads, tables, head_bias):
    parts = [vgrads[0][11:14].reshape(-1)]
    for layer in range(LAYERS):
        parts += [vgrads[layer][:11].reshape(-1), tables[layer].reshape(-1)]
    return jnp.concatenate([*parts, vgrads[1][11:13].reshape(-1), head_bias[:CLASSES]])


def group_parts(group, conv, qkv, proj, up, down, head):
    layer = [m[group] for m in (qkv, proj, up, down)]
    return [conv] + layer if group == 0 else layer + [head]


def factor_rows(group, *factors):
    out = []
    for f in group_parts(group, *factors):
        out.append(jnp.pad(f.T, ((0, 0), (0, CPAD - CLASSES))) if f.shape[0] == CLASSES else f.T)
    return jnp.concatenate(out, axis=1)


def split_right(right):
    widths = [(D, 3 * D, D, FF, D), (3 * D, D, FF, D, CPAD)]
    cut, at = [], 0
    for row in widths:
        for w in row:
            cut.append(right[:, at : at + w].T)
            at += w
    layer = [jnp.stack([cut[1 + i], cut[5 + i]]) for i in range(4)]
    return (cut[0], *layer, cut[9][:CLASSES])


def padded_rows(values, rows, fill):
    values = jnp.pad(values, (0, rows - values.shape[0]), constant_values=fill)
    return jnp.broadcast_to(values[:, None], (rows, 128))


def step(mesh, args):
    (
        features, labels, counts, tables, *rest
    ) = args
    weights, moms, errs, facs = rest[0:6], rest[6:12], rest[12:18], rest[18:24]
    small_params, small_mom = rest[24:]
    reps = mesh.shape["rep"]
    quick = mesh.shape["fsdp"] == SHARDS and reps & (reps - 1) == 0
    slots = features.shape[0]
    items = 2 if slots % 2 == 0 else 1
    rows = -(-slots // 16) * 16

    if quick:
        me = lax.axis_index("fsdp").astype(jnp.int32)[None]
        low = [w.astype(BF16) for w in weights]
        count = counts[0, 0].astype(F32)
        first = pack(group_parts(0, *low))
        cut, end = SPLIT[0], first.shape[0]
        with_count = jnp.concatenate([first[:cut], jnp.broadcast_to(count.astype(BF16), (16, D))], axis=0)
        sources0 = gather_halves(with_count, first[cut:], cut, end)
        replica_count = jnp.sum(sources0[0][0][:, cut, 0].astype(F32))
        replica_count = replica_count + jnp.sum(sources0[1][0][:, cut, 0].astype(F32))
        item_count = sum_replicas(jnp.broadcast_to(replica_count, (8, 128)), reps)[0, 0]
        second = pack(group_parts(1, *low))
        sources1 = gather_direct(second)
    else:
        me = jnp.zeros((1,), jnp.int32)
        item_count = lax.psum(counts[0, 0].astype(F32), ("rep", "fsdp"))
        sides = [lax.all_gather(w.astype(BF16), "fsdp", axis=w.ndim - 2, tiled=True) for w in weights]
        sources = []
        for group in range(2):
            parts = group_parts(group, *sides)
            shards = [pack([p.reshape(SHARDS, -1, p.shape[1])[s] for p in parts]) for s in range(SHARDS)]
            sources.append([(jnp.stack(shards), 0, shards[0].shape[0], tuple(range(SHARDS)))])
        sources0, sources1 = sources

    conv_vec, layer_vecs, final, bias_tables, head_bias = small_blocks(small_params)
    bias = make_bias(bias_tables)
    patches = make_patches(features)
    zero = forward_zero(me, patches, sources0, layer_vecs[0], conv_vec, bias, items)
    live = (jnp.arange(slots, dtype=jnp.int32) < counts[0, 0]).astype(F32)
    one = forward_one(
        me,
        zero.hidden,
        sources1,
        layer_vecs[1],
        final,
        bias,
        head_bias,
        padded_rows(labels, rows, -1),
        padded_rows(live, rows, 0.0),
        jnp.broadcast_to(1.0 / item_count, (rows, 128)),
        items,
    )
    fac_rows = [factor_rows(group, *facs) for group in range(2)]
    if quick:
        err = [e[0] for e in errs]
        packed_err = [pack(group_parts(group, *err)) for group in range(2)]
    else:
        packed_err = [jnp.zeros((pieces_of(SHARDS, group)[1], D), F32) for group in range(2)]
    back_one = backward_one(me, zero.hidden, one, layer_vecs[1], final, packed_err[1], fac_rows[1], items)
    back_zero = backward_zero(
        me, back_one.d_hidden, zero, patches, layer_vecs[0], conv_vec, packed_err[0], fac_rows[0], items
    )
    tables_grad = [table_grad(back_zero.bgrad, 0), table_grad(back_one.bgrad, 1)]
    if not quick:
        grads = [whole_matrices(group, b.whole) for group, b in ((0, back_zero), (1, back_one))]
        small = small_vector((back_zero.vgrad, back_one.vgrad), tables_grad, one.head_bias_grad[0])
        loss = lax.psum(one.loss[0, 0], ("rep", "fsdp"))
        return (loss, item_count, *general_tail(grads, weights, moms, errs, facs, small, small_params, small_mom))

    received = []
    for group, back in ((0, back_zero), (1, back_one)):
        received.append([swap(getattr(back, f"sent{j}"), j) for j in range(1, SHARDS)])
    left = jnp.concatenate([back_zero.left, back_one.left], axis=1)
    lanes = left.shape[1]
    left = sum_replicas(sum_replica(pad_lanes(left, -(-lanes // 256) * 256)), reps)
    left = join_halves(left, swap(left, 1))[:, :lanes]
    factors = right_factors(me, left, back_zero.whole, back_one.whole)
    payload = jnp.concatenate(
        [
            factors.right,
            back_zero.vgrad.reshape(8, 512),
            back_one.vgrad.reshape(8, 512),
            one.head_bias_grad.reshape(8, 128),
            pad_lanes(tables_grad[0].reshape(HEADS, RB), 256),
            pad_lanes(tables_grad[1].reshape(HEADS, RB), 256),
            one.loss,
        ],
        axis=1,
    )
    mine = sum_replica(payload)
    every = sum_replicas(mine, reps)
    both = jnp.stack([mine, every])
    both = join_halves(both, swap(both, 1))
    width = factors.right.shape[1]
    right_mine, summed = both[0, :, :width], both[1]
    right_all = summed[:, :width]
    updated = apply_update(
        me,
        weights,
        moms,
        right_mine,
        right_all,
        (factors.basis0, factors.basis1),
        (back_zero.own, back_one.own),
        received,
    )
    vgrads = [summed[:, width + 512 * i : width + 512 * (i + 1)].reshape(16, D) for i in range(2)]
    at = width + 1024
    head_bias_grad = summed[:, at : at + 128].reshape(-1)
    table_sums = [summed[:, at + 128 + 256 * i : at + 128 + 256 * i + RB] for i in range(2)]
    loss = summed[0, at + 640]
    new_small_mom = MOMENTUM * small_mom + small_vector(vgrads, table_sums, head_bias_grad)
    names = [n for n, _ in UPDATED]
    return (
        loss,
        item_count,
        *[getattr(updated, "new_" + n) for n in names],
        *[getattr(updated, "new_mom_" + n) for n in names],
        *[getattr(updated, "err_" + n) for n in names],
        *split_right(right_all),
        small_params - SMALL_RATE * new_small_mom,
        new_small_mom,
    )


def whole_matrices(group, packed):
    out = {}
    for name, (at, rows, blocks) in pieces_of(SHARDS, group)[0].items():
        cols = [packed[:, at + c * rows : at + (c + 1) * rows, :].reshape(SHARDS * rows, D) for c in range(blocks)]
        out[name] = jnp.concatenate(cols, axis=1)
    return out


def orthonormal(product, gram_mat):
    lower_tri = jnp.linalg.cholesky(gram_mat)
    return jnp.swapaxes(
        jax.scipy.linalg.solve_triangular(lower_tri, jnp.swapaxes(product, 1, 2), lower=True), 1, 2
    )


def general_tail(grads, weights, moms, errs, facs, small, small_params, small_mom):
    layer = [jnp.stack([grads[g][n] for g in range(2)]) for n in MATRIX_NAMES]
    wholes = [grads[0]["conv"][None], *layer, grads[1]["head"][None, :, :CLASSES]]
    lift = lambda xs: [xs[0][None], *xs[1:5], xs[5][None]]
    weights, moms, facs = lift(weights), lift(moms), lift(facs)
    errors = [errs[0], *[e[0] for e in errs[1:5]], errs[5]]
    merged = [
        lax.psum_scatter(g, "fsdp", scatter_dimension=1, tiled=True) + e for g, e in zip(wholes, errors)
    ]
    lefts = lax.psum(
        [jnp.einsum("bio,bok->bik", m, f, precision=PRECISE) for m, f in zip(merged, facs)], "rep"
    )
    grams = lax.psum([jnp.einsum("bik,bil->bkl", p, p, precision=PRECISE) for p in lefts], "fsdp")
    bases = [orthonormal(p, g) for p, g in zip(lefts, grams)]
    local = [jnp.einsum("bio,bik->bok", m, b, precision=PRECISE) for m, b in zip(merged, bases)]
    mine = lax.psum([*local, small], "fsdp")
    every = lax.psum(mine, "rep")
    product = lambda b, q: jnp.einsum("bik,bok->bio", b, q, precision=PRECISE)
    new_errs = [m - product(b, q) for m, b, q in zip(merged, bases, mine)]
    new_moms = [MOMENTUM * m + product(b, q) for m, b, q in zip(moms, bases, every)]
    new_weights = [w - LEARN_RATE * m for w, m in zip(weights, new_moms)]
    drop = lambda xs: [xs[0][0], *xs[1:5], xs[5][0]]
    new_small_mom = MOMENTUM * small_mom + every[6]
    return (
        *drop(new_weights),
        *drop(new_moms),
        new_errs[0],
        *[e[None] for e in new_errs[1:5]],
        new_errs[5],
        *drop(every[:6]),
        small_params - SMALL_RATE * new_small_mom,
        new_small_mom,
    )


def solution(mesh):
    rows, mids = P("fsdp", None), P(None, "fsdp", None)
    matrices = (rows, mids, mids, mids, mids, rows)
    errors = (
        P("rep", "fsdp", None),
        *[P("rep", None, "fsdp", None)] * 4,
        P("rep", "fsdp", None),
    )
    return jax.shard_map(
        lambda *args: step(mesh, args),
        mesh=mesh,
        in_specs=(
            P(("rep", "fsdp"), None, None, None),
            P(("rep", "fsdp")),
            P("rep", "fsdp"),
            P(),
            *matrices,
            *matrices,
            *errors,
            *[P()] * 8,
        ),
        out_specs=(P(), P(), *matrices, *matrices, *errors, *[P()] * 8),
        check_vma=False,
    )
```

time: 923 us -> 412 us (0.45)
  matrix products: 264 us -> 2.68 us
  Pallas kernels: 0 us -> 251 us
  blocking collectives: 181 us -> 0 us
  other arithmetic: 180 us -> 15.4 us
  waiting for transfers between devices: 177 us -> 65.6 us
  local copies, waits for them, and re-layouts: 96.6 us -> 26.4 us
  starting transfers between devices: 0.29 us -> 42.1 us
  between operations: 18.2 us -> 4.82 us
    dot_general x79 -> x3, matrix products: 263 us -> 2.68 us  [the longest x2 1.76 us: table_grad(): jnp.einsum('pd,hpe->hde', jnp.asarray(rows_hot), rows.reshape(HEADS, GRID...]
    pallas_call x0 -> x10, Pallas kernels: none -> 251 us  [the longest x6 220 us: call(): pl.pallas_call(body, grid_spec=pltpu.PrefetchScalarGridSpec(num_scalar_pr...]
    reduce_sum x33 -> x2, other arithmetic: 114 us -> 1.28 us  [the longest x1 0.68 us: step(): jnp.sum(sources0[1][0][:, cut, 0].astype(F32))]
    all_gather x10 -> x0, blocking collectives: 98.2 us -> none  [the longest x2 20.1 us: body(): lax.all_gather(proj_weight[layer_idx].astype(jnp.bfloat16), 'fsdp', axis=...]
    psum x2 -> x0, waiting for transfers between devices: 91.1 us -> none  [the longest x1 51.5 us: body(): lax.psum((local_q[0], local_q[1], local_q[2], local_q[3], local_q[4], loc...]
    reduce_scatter x6 -> x0, waiting for transfers between devices: 85.2 us -> none  [the longest x1 40.4 us: body(): lax.psum_scatter(stacks[2], 'fsdp', scatter_dimension=1, tiled=True)]
    psum x3 -> x0, blocking collectives: 82.3 us -> none  [the longest x1 39.9 us: body(): lax.psum((jnp.sum(live_mask * losses), jnp.sum(live_mask)), ('rep', 'fsdp'))]
    ppermute x0 -> x41, waiting for transfers between devices: none -> 65.6 us  [the longest x31 39.8 us: swap(): return lax.ppermute(x, 'fsdp', [(i, i ^ offset) for i in range(SHARDS)])]
  transfers between devices with their start and end apart: 8 -> 41, of which waited for: 5 -> 17; matrix products, arithmetic and copies ran while one was open for 17% -> 6% of each run, Pallas kernels for 0% -> 21%
where the time goes in v1:
time: 412 us; the launch traced here: 408 us
  Pallas kernels  251 us (61%)
  waiting for transfers between devices  65.6 us (16%)
  starting transfers between devices  42.1 us (10%)
  local copies, waits for them, and re-layouts  26.4 us (6%)
  other arithmetic  15.4 us (4%)
  between operations  4.82 us (1%)
    pallas_call x6, Pallas kernels, call(): pl.pallas_call(body, grid_spec=pltpu.PrefetchScalarGridSpec(num_scalar_pr...  220 us
    ppermute x31, waiting for transfers between devices, swap(): return lax.ppermute(x, 'fsdp', [(i, i ^ offset) for i in range(SHARDS)])  39.8 us
    ppermute x31, starting transfers between devices, swap(): return lax.ppermute(x, 'fsdp', [(i, i ^ offset) for i in range(SHARDS)])  27.9 us
    ppermute x4, waiting for transfers between devices, swap_by_core(): lax.ppermute(x, 'fsdp', [(i, i ^ (odd if i & 1 else even)) for i in range...  14.3 us
    pallas_call x2, Pallas kernels, table_grad(): pl.pallas_call(table_grad_kernel, grid=(1,), in_specs=[whole((1, HEADS *...  12.6 us
    ppermute x6, waiting for transfers between devices, swap_rep(): return lax.ppermute(x, 'rep', [(i, i ^ offset) for i in range(reps)])  11.5 us
    ppermute x6, starting transfers between devices, swap_rep(): return lax.ppermute(x, 'rep', [(i, i ^ offset) for i in range(reps)])  9.95 us
    pallas_call x1, Pallas kernels, make_bias(): pl.pallas_call(bias_kernel, grid=(LAYERS,), in_specs=[pl.BlockSpec((1, HE...  9.35 us
  transfers between devices with their start and end apart: 41, of which 17 were waited for; matrix products, arithmetic and copies ran while one was open for 6% of the time, Pallas kernels for 21%

profile of v1, /device:TPU:0, one launch (start us, length us, event | category | flops | bytes accessed | tf_op | source)
XLA Modules:
  0.0 408.2 jit_solution(10473902442217922373)
XLA Ops:
  13.2 2.5 collective-permute-start.7
  17.5 1.8 collective-permute-start
  25.0 4.7 %collective-permute-done.3 = bf16[1,224,256]{2,1,0:T(8,128)(2,1)S(1)} collective-permute-done((bf16[1,224,256]{2,1,0:T(8,128)(2,1)S(1)}, bf16[1,224,256]{2,1,0:T(8,128)(2,1)S(1)}, u32[]{:S(2)}, u32[]{:S(2)}) %collective-permute-start.3) | collective-permute-done | bytes 114720 | tf_op jit(solution)/shard_map/ppermute | solution.py:975
  29.8 2.0 collective-permute-start.4
  31.8 3.4 collective-permute-done.1
  40.1 1.9 collective-permute-start.13
  43.8 2.8 collective-permute-start.14
  54.0 9.1 %patches.1.refs_1_.refs_3_ = bf16[12,2,224,384]{3,2,1,0:T(8,128)(2,1)} custom-call(bf16[12,28,28,128]{3,2,1,0:T(8,128)(2,1)} %feat_ref.1), custom_call_target="tpu_custom_call" | custom-call | tf_op jit(solution)/shard_map/patches/pallas_call | solution.py:208
  65.6 9.4 %bias.1.refs_8_.refs_12_ = f32[2,8,224,128]{3,2,1,0:T(8,128)} custom-call(f32[2,112,128]{2,1,0:T(8,128)} %reshape.152.rows_ref, f32[2,16,128,128]{3,2,1,0:T(8,128)} %constant.40.clone.shift_ref, f32[2,224,128]{2,1,0:T(8,128)} %constant.41.clone.mask_ref), custom_call_target="tpu_custom_call" | custom-call | tf_op jit(solution)/shard_map/bias/pallas_call | solution.py:243
  74.9 54.6 %forward_zero.1 = (f32[2688,256]{1,0:T(8,128)}, f32[2688,256]{1,0:T(8,128)}, bf16[2688,768]{1,0:T(8,128)(2,1)}, f32[12,224,1024]{2,1,0:T(8,128)}, bf16[2688,256]...) custom-call(s32[1]{0:T(128)} %bitcast.refs_0_, ...), custom_call_target="tpu_custom_call" | custom-call | tf_op jit(solution)/shard_map/forward_zero/pallas_call | solution.py:174
  132.8 42.9 %forward_one.1 = (f32[2688,256]{1,0:T(8,128)}, bf16[2688,768]{1,0:T(8,128)(2,1)}, f32[12,224,1024]{2,1,0:T(8,128)}, bf16[2688,256]{1,0:T(8,128)(2,1)}, f32[2688,...) custom-call(s32[1]{0:T(128)} %bitcast.refs_0_, ...), custom_call_target="tpu_custom_call" | custom-call | tf_op jit(solution)/shard_map/forward_one/pallas_call | solution.py:174
  175.7 46.0 %backward_one.1 = (f32[2688,256]{1,0:T(8,128)}, f32[16,256]{1,0:T(8,128)}, f32[1792,128]{1,0:T(8,128)}, f32[8,448,256]{2,1,0:T(8,128)}, f32[448,256]{1,0:T(8,128...) custom-call(s32[1]{0:T(128)} %bitcast.refs_0_, ...), custom_call_target="tpu_custom_call" | custom-call | tf_op jit(solution)/shard_map/backward_one/pallas_call | solution.py:174
  221.8 63.8 %backward_zero.1 = (f32[16,256]{1,0:T(8,128)}, f32[1792,128]{1,0:T(8,128)}, f32[8,464,256]{2,1,0:T(8,128)}, f32[464,256]{1,0:T(8,128)}, bf16[464,256]{1,0:T(8,12...) custom-call(s32[1]{0:T(128)} %bitcast.refs_0_, ...), custom_call_target="tpu_custom_call" | custom-call | tf_op jit(solution)/shard_map/backward_zero/pallas_call | solution.py:174
  290.3 2.9 collective-permute-done.16
  294.8 2.9 collective-permute-done.17
  297.6 1.6 collective-permute-start.18
  299.3 6.2 %table_grad.2 = f32[1,112,128]{2,1,0:T(8,128)} custom-call(f32[1,1792,128]{2,1,0:T(8,128)} %bitcast.174, f32[1,16,128,128]{3,2,1,0:T(8,128)} %constant.77.shift_ref), custom_call_target="tpu_custom_call" | custom-call | tf_op jit(solution)/shard_map/table_grad/pallas_call | solution.py:269
  306.5 2.3 collective-permute-start.19
  309.6 6.4 %table_grad.3 = f32[1,112,128]{2,1,0:T(8,128)} custom-call(f32[1,1792,128]{2,1,0:T(8,128)} %bitcast.173, f32[1,16,128,128]{3,2,1,0:T(8,128)} %constant.78.shift_ref), custom_call_target="tpu_custom_call" | custom-call | tf_op jit(solution)/shard_map/table_grad/pallas_call | solution.py:269
  319.3 7.7 %right_factors.1 = (f32[8,5376]{1,0:T(8,128)}, f32[8,8,336]{2,1,0:T(8,128)}, f32[8,8,224]{2,1,0:T(8,128)}) custom-call(s32[1]{0:T(128)} %bitcast.refs_0_, f32[8,4480]{1,0:T(8,128)} %pad_maximum_fusion.6.refs_1_, f32[8,464,256]{2,1,0:T(8,128)} %get-tuple-element.129.refs_2_, f32[8,448,256]{2,1,0:T(8,128)} %get-tuple-element.130.refs_3_), custom_call_target="tpu_custom_call" | custom-call | tf_op jit(solution)/shard_map/right_factors/pallas_call | solution.py:174
  332.1 4.3 %collective-permute-done.22 = f32[8,3584]{1,0:T(8,128)S(1)} collective-permute-done((f32[8,3584]{1,0:T(8,128)S(1)}, f32[8,3584]{1,0:T(8,128)S(1)}, u32[]{:S(2)}, u32[]{:S(2)}) %collective-permute-start.22) | collective-permute-done | bytes 114720 | tf_op jit(solution)/shard_map/ppermute | solution.py:979
  337.0 4.3 %collective-permute-done.23 = f32[8,3584]{1,0:T(8,128)S(1)} collective-permute-done((f32[8,3584]{1,0:T(8,128)S(1)}, f32[8,3584]{1,0:T(8,128)S(1)}, u32[]{:S(2)}, u32[]{:S(2)}) %collective-permute-start.23) | collective-permute-done | bytes 114720 | tf_op jit(solution)/shard_map/ppermute | solution.py:979
  341.8 4.3 %collective-permute-done.24 = f32[8,3584]{1,0:T(8,128)S(1)} collective-permute-done((f32[8,3584]{1,0:T(8,128)S(1)}, f32[8,3584]{1,0:T(8,128)S(1)}, u32[]{:S(2)}, u32[]{:S(2)}) %collective-permute-start.24) | collective-permute-done | bytes 114720 | tf_op jit(solution)/shard_map/ppermute | solution.py:983
  346.9 6.1 %collective-permute-done.25 = f32[8,3584]{1,0:T(8,128)S(1)} collective-permute-done((f32[8,3584]{1,0:T(8,128)S(1)}, f32[8,3584]{1,0:T(8,128)S(1)}, u32[]{:S(2)}, u32[]{:S(2)}) %collective-permute-start.25) | collective-permute-done | bytes 114720 | tf_op jit(solution)/shard_map/ppermute | solution.py:983
  359.1 3.2 collective-permute-done.35.refs_27_
  362.4 4.0 collective-permute-done.36.refs_28_
  366.9 2.8 collective-permute-start.40
  371.7 5.6 %collective-permute-done.39.refs_31_ = bf16[448,256]{1,0:T(8,128)(2,1)S(1)} collective-permute-done((bf16[448,256]{1,0:T(8,128)(2,1)}, bf16[448,256]{1,0:T(8,128)(2,1)S(1)}, u32[]{:S(2)}, u32[]{:S(2)}) %collective-permute-start.39) | collective-permute-done | bytes 229408 | tf_op jit(solution)/shard_map/ppermute | solution.py:975
  378.8 2.6 collective-permute-done.40.refs_32_
  381.3 1.8 collective-permute-start.31
  387.8 14.2 %collective-permute-done.31.refs_23_ = bf16[464,256]{1,0:T(8,128)(2,1)S(1)} collective-permute-done((bf16[464,256]{1,0:T(8,128)(2,1)S(1)}, bf16[464,256]{1,0:T(8,128)(2,1)S(1)}, u32[]{:S(2)}, u32[]{:S(2)}) %collective-permute-start.31) | collective-permute-done | bytes 237600 | tf_op jit(solution)/shard_map/ppermute | solution.py:975
  402.8 5.1 %apply_update.1 = (f32[144,256]{1,0:T(8,128)}, f32[2,32,768]{2,1,0:T(8,128)}, f32[2,32,256]{2,1,0:T(8,128)}, f32[2,32,768]{2,1,0:T(8,128)}, f32[2,96,256]{2,1,0:...) custom-call(s32[1]{0:T(128)} %bitcast.refs_0_, ...), custom_call_target="tpu_custom_call" | custom-call | tf_op jit(solution)/shard_map/apply_update/pallas_call | solution.py:174
  (307 shorter events, 70.2 us)
Async XLA Ops:
  12.8 33.9 %collective-permute-start.6 = (bf16[448,256]{1,0:T(8,128)(2,1)}, bf16[448,256]{1,0:T(8,128)(2,1)S(1)}, u32[]{:S(2)}, u32[]{:S(2)}) collective-permute-start(bf16[448,256]{1,0:T(8,128)(2,1)} %constant_dynamic-update-slice_fusion.5), channel_id=1, source_target_pairs={{0,1},{1,0},{2,3},{3,2},{4,5},{5,4},{6,7},{7,6},{8,9},{9,8},{10,11... | collective-permute-start | bytes 688136 | tf_op jit(solution)/shard_map/ppermute | solution.py:975
  13.2 35.0 %collective-permute-start.7 = (bf16[448,256]{1,0:T(8,128)(2,1)}, bf16[448,256]{1,0:T(8,128)(2,1)}, u32[]{:S(2)}, u32[]{:S(2)}) collective-permute-start(bf16[448,256]{1,0:T(8,128)(2,1)} %constant_dynamic-update-slice_fusion.5), channel_id=1, source_target_pairs={{0,2},{1,3},{2,0},{3,1},{4,6},{5,7},{6,4},{7,5},{8,10},{9,11},{10,... | collective-permute-start | bytes 688136 | tf_op jit(solution)/shard_map/ppermute | solution.py:975
  15.7 115.1 %collective-permute-start.8 = (bf16[448,256]{1,0:T(8,128)(2,1)}, bf16[448,256]{1,0:T(8,128)(2,1)}, u32[]{:S(2)}, u32[]{:S(2)}) collective-permute-start(bf16[448,256]{1,0:T(8,128)(2,1)} %constant_dynamic-update-slice_fusion.5), channel_id=1, source_target_pairs={{0,3},{1,2},{2,1},{3,0},{4,7},{5,6},{6,5},{7,4},{8,11},{9,10},{10,... | collective-permute-start | bytes 688136 | tf_op jit(solution)/shard_map/ppermute | solution.py:975
  17.5 6.5 %collective-permute-start = (bf16[1,256,256]{2,1,0:T(8,128)(2,1)S(1)}, bf16[1,256,256]{2,1,0:T(8,128)(2,1)S(1)}, u32[]{:S(2)}, u32[]{:S(2)}) collective-permute-start(bf16[1,256,256]{2,1,0:T(8,128)(2,1)S(1)} %fusion.10), channel_id=1, source_target_pairs={{0,4},{1,5},{2,6},{3,7},{4,0},{5,1},{6,2},{7,3},{8,12},{9,13},{10,... | collective-permute-start | bytes 393224 | tf_op jit(solution)/shard_map/ppermute | solution.py:975
  19.3 10.5 %collective-permute-start.3 = (bf16[1,224,256]{2,1,0:T(8,128)(2,1)S(1)}, bf16[1,224,256]{2,1,0:T(8,128)(2,1)S(1)}, u32[]{:S(2)}, u32[]{:S(2)}) collective-permute-start(bf16[1,224,256]{2,1,0:T(8,128)(2,1)S(1)} %bitcast.175), channel_id=1, source_target_pairs={{0,2},{1,3},{2,0},{3,1},{4,6},{5,7},{6,4},{7,5},{8,10},{9,11},{10,... | collective-permute-start | bytes 344072 | tf_op jit(solution)/shard_map/ppermute | solution.py:975
  24.0 11.2 %collective-permute-start.1 = (bf16[2,256,256]{2,1,0:T(8,128)(2,1)S(1)}, bf16[2,256,256]{2,1,0:T(8,128)(2,1)S(1)}, u32[]{:S(2)}, u32[]{:S(2)}) collective-permute-start(bf16[2,256,256]{2,1,0:T(8,128)(2,1)S(1)} %pad_maximum_fusion.2), channel_id=1, source_target_pairs={{0,2},{1,3},{2,0},{3,1},{4,6},{5,7},{6,4},{7,5},{8,10},{9,11},{10,... | collective-permute-start | bytes 786440 | tf_op jit(solution)/shard_map/ppermute | solution.py:975
  29.8 7.3 %collective-permute-start.4 = (bf16[2,224,256]{2,1,0:T(8,128)(2,1)S(1)}, bf16[2,224,256]{2,1,0:T(8,128)(2,1)S(1)}, u32[]{:S(2)}, u32[]{:S(2)}) collective-permute-start(bf16[2,224,256]{2,1,0:T(8,128)(2,1)S(1)} %pad_maximum_fusion.3), channel_id=1, source_target_pairs={{0,4},{1,5},{2,6},{3,7},{4,0},{5,1},{6,2},{7,3},{8,12},{9,13},{10,... | collective-permute-start | bytes 688136 | tf_op jit(solution)/shard_map/ppermute | solution.py:975
  37.2 11.1 %collective-permute-start.5 = (bf16[4,224,256]{2,1,0:T(8,128)(2,1)S(1)}, bf16[4,224,256]{2,1,0:T(8,128)(2,1)S(1)}, u32[]{:S(2)}, u32[]{:S(2)}) collective-permute-start(bf16[4,224,256]{2,1,0:T(8,128)(2,1)S(1)} %pad_maximum_fusion.1.refs_4_), channel_id=1, source_target_pairs={{0,1},{1,0},{2,3},{3,2},{4,5},{5,4},{6,7},{7,6},{8,9},{9,8},{10,11... | collective-permute-start | bytes 1376264 | tf_op jit(solution)/shard_map/ppermute | solution.py:975
  43.8 6.0 %collective-permute-start.14 = (f32[8,128]{1,0:T(8,128)S(1)}, f32[8,128]{1,0:T(8,128)S(1)}, u32[]{:S(2)}, u32[]{:S(2)}) collective-permute-start(f32[8,128]{1,0:T(8,128)S(1)} %broadcast_add_fusion), channel_id=1, source_target_pairs={{0,16},{8,24},{16,0},{24,8},{1,17},{9,25},{17,1},{25,9},{2,18},{10... | collective-permute-start | bytes 12296 | tf_op jit(solution)/shard_map/ppermute | solution.py:983
  46.7 84.1 %collective-permute-start.9 = (bf16[448,256]{1,0:T(8,128)(2,1)}, bf16[448,256]{1,0:T(8,128)(2,1)}, u32[]{:S(2)}, u32[]{:S(2)}) collective-permute-start(bf16[448,256]{1,0:T(8,128)(2,1)} %constant_dynamic-update-slice_fusion.5), channel_id=1, source_target_pairs={{0,4},{1,5},{2,6},{3,7},{4,0},{5,1},{6,2},{7,3},{8,12},{9,13},{10,... | collective-permute-start | bytes 688136 | tf_op jit(solution)/shard_map/ppermute | solution.py:975
  48.2 82.6 %collective-permute-start.10 = (bf16[448,256]{1,0:T(8,128)(2,1)}, bf16[448,256]{1,0:T(8,128)(2,1)}, u32[]{:S(2)}, u32[]{:S(2)}) collective-permute-start(bf16[448,256]{1,0:T(8,128)(2,1)} %constant_dynamic-update-slice_fusion.5), channel_id=1, source_target_pairs={{0,5},{1,4},{2,7},{3,6},{4,1},{5,0},{6,3},{7,2},{8,13},{9,12},{10,... | collective-permute-start | bytes 688136 | tf_op jit(solution)/shard_map/ppermute | solution.py:975
  48.3 82.6 %collective-permute-start.11 = (bf16[448,256]{1,0:T(8,128)(2,1)}, bf16[448,256]{1,0:T(8,128)(2,1)}, u32[]{:S(2)}, u32[]{:S(2)}) collective-permute-start(bf16[448,256]{1,0:T(8,128)(2,1)} %constant_dynamic-update-slice_fusion.5), channel_id=1, source_target_pairs={{0,6},{1,7},{2,4},{3,5},{4,2},{5,3},{6,0},{7,1},{8,14},{9,15},{10,... | collective-permute-start | bytes 688136 | tf_op jit(solution)/shard_map/ppermute | solution.py:975
  49.8 81.1 %collective-permute-start.12 = (bf16[448,256]{1,0:T(8,128)(2,1)}, bf16[448,256]{1,0:T(8,128)(2,1)}, u32[]{:S(2)}, u32[]{:S(2)}) collective-permute-start(bf16[448,256]{1,0:T(8,128)(2,1)} %constant_dynamic-update-slice_fusion.5), channel_id=1, source_target_pairs={{0,7},{1,6},{2,5},{3,4},{4,3},{5,2},{6,1},{7,0},{8,15},{9,14},{10,... | collective-permute-start | bytes 688136 | tf_op jit(solution)/shard_map/ppermute | solution.py:975
  297.6 8.8 %collective-permute-start.18 = (f32[8,2304]{1,0:T(8,128)S(1)}, f32[8,2304]{1,0:T(8,128)S(1)}, u32[]{:S(2)}, u32[]{:S(2)}) collective-permute-start(f32[8,2304]{1,0:T(8,128)S(1)} %add.67), channel_id=1, source_target_pairs={{0,8},{8,0},{16,24},{24,16},{1,9},{9,1},{17,25},{25,17},{2,10},{10... | collective-permute-start | bytes 221192 | tf_op jit(solution)/shard_map/ppermute | solution.py:983
  306.5 10.6 %collective-permute-start.19 = (f32[8,2304]{1,0:T(8,128)S(1)}, f32[8,2304]{1,0:T(8,128)S(1)}, u32[]{:S(2)}, u32[]{:S(2)}) collective-permute-start(f32[8,2304]{1,0:T(8,128)S(1)} %add.68), channel_id=1, source_target_pairs={{0,16},{8,24},{16,0},{24,8},{1,17},{9,25},{17,1},{25,9},{2,18},{10... | collective-permute-start | bytes 221192 | tf_op jit(solution)/shard_map/ppermute | solution.py:983
  331.5 4.9 %collective-permute-start.22 = (f32[8,3584]{1,0:T(8,128)S(1)}, f32[8,3584]{1,0:T(8,128)S(1)}, u32[]{:S(2)}, u32[]{:S(2)}) collective-permute-start(f32[8,3584]{1,0:T(8,128)S(1)} %select_add_fusion), channel_id=1, source_target_pairs={{0,2},{1,5},{2,0},{3,7},{4,6},{5,1},{6,4},{7,3},{8,10},{9,13},{10,... | collective-permute-start | bytes 344072 | tf_op jit(solution)/shard_map/ppermute | solution.py:979
  336.4 4.9 %collective-permute-start.23 = (f32[8,3584]{1,0:T(8,128)S(1)}, f32[8,3584]{1,0:T(8,128)S(1)}, u32[]{:S(2)}, u32[]{:S(2)}) collective-permute-start(f32[8,3584]{1,0:T(8,128)S(1)} %add.71), channel_id=1, source_target_pairs={{0,4},{1,3},{2,6},{3,1},{4,0},{5,7},{6,2},{7,5},{8,12},{9,11},{10,... | collective-permute-start | bytes 344072 | tf_op jit(solution)/shard_map/ppermute | solution.py:979
  341.3 4.9 %collective-permute-start.24 = (f32[8,3584]{1,0:T(8,128)S(1)}, f32[8,3584]{1,0:T(8,128)S(1)}, u32[]{:S(2)}, u32[]{:S(2)}) collective-permute-start(f32[8,3584]{1,0:T(8,128)S(1)} %add.72), channel_id=1, source_target_pairs={{0,8},{8,0},{16,24},{24,16},{1,9},{9,1},{17,25},{25,17},{2,10},{10... | collective-permute-start | bytes 344072 | tf_op jit(solution)/shard_map/ppermute | solution.py:983
  346.2 6.9 %collective-permute-start.25 = (f32[8,3584]{1,0:T(8,128)S(1)}, f32[8,3584]{1,0:T(8,128)S(1)}, u32[]{:S(2)}, u32[]{:S(2)}) collective-permute-start(f32[8,3584]{1,0:T(8,128)S(1)} %add.73), channel_id=1, source_target_pairs={{0,16},{8,24},{16,0},{24,8},{1,17},{9,25},{17,1},{25,9},{2,18},{10... | collective-permute-start | bytes 344072 | tf_op jit(solution)/shard_map/ppermute | solution.py:983
  353.2 30.0 %collective-permute-start.27 = (bf16[464,256]{1,0:T(8,128)(2,1)S(1)}, bf16[464,256]{1,0:T(8,128)(2,1)S(1)}, u32[]{:S(2)}, u32[]{:S(2)}) collective-permute-start(bf16[464,256]{1,0:T(8,128)(2,1)S(1)} %copy-done.48), channel_id=1, source_target_pairs={{0,1},{1,0},{2,3},{3,2},{4,5},{5,4},{6,7},{7,6},{8,9},{9,8},{10,11... | collective-permute-start | bytes 712712 | tf_op jit(solution)/shard_map/ppermute | solution.py:975
  353.7 8.6 %collective-permute-start.35 = (bf16[448,256]{1,0:T(8,128)(2,1)}, bf16[448,256]{1,0:T(8,128)(2,1)S(1)}, u32[]{:S(2)}, u32[]{:S(2)}) collective-permute-start(bf16[448,256]{1,0:T(8,128)(2,1)} %get-tuple-element.150), channel_id=1, source_target_pairs={{0,2},{1,3},{2,0},{3,1},{4,6},{5,7},{6,4},{7,5},{8,10},{9,11},{10,... | collective-permute-start | bytes 688136 | tf_op jit(solution)/shard_map/ppermute | solution.py:975
  354.3 12.1 %collective-permute-start.36 = (bf16[448,256]{1,0:T(8,128)(2,1)}, bf16[448,256]{1,0:T(8,128)(2,1)S(1)}, u32[]{:S(2)}, u32[]{:S(2)}) collective-permute-start(bf16[448,256]{1,0:T(8,128)(2,1)} %get-tuple-element.151), channel_id=1, source_target_pairs={{0,3},{1,2},{2,1},{3,0},{4,7},{5,6},{6,5},{7,4},{8,11},{9,10},{10,... | collective-permute-start | bytes 688136 | tf_op jit(solution)/shard_map/ppermute | solution.py:975
  355.5 11.4 %collective-permute-start.37 = (bf16[448,256]{1,0:T(8,128)(2,1)}, bf16[448,256]{1,0:T(8,128)(2,1)S(1)}, u32[]{:S(2)}, u32[]{:S(2)}) collective-permute-start(bf16[448,256]{1,0:T(8,128)(2,1)} %get-tuple-element.152), channel_id=1, source_target_pairs={{0,4},{1,5},{2,6},{3,7},{4,0},{5,1},{6,2},{7,3},{8,12},{9,13},{10,... | collective-permute-start | bytes 688136 | tf_op jit(solution)/shard_map/ppermute | solution.py:975
  358.5 25.3 %collective-permute-start.28 = (bf16[464,256]{1,0:T(8,128)(2,1)S(1)}, bf16[464,256]{1,0:T(8,128)(2,1)S(1)}, u32[]{:S(2)}, u32[]{:S(2)}) collective-permute-start(bf16[464,256]{1,0:T(8,128)(2,1)S(1)} %copy-done.47), channel_id=1, source_target_pairs={{0,2},{1,3},{2,0},{3,1},{4,6},{5,7},{6,4},{7,5},{8,10},{9,11},{10,... | collective-permute-start | bytes 712712 | tf_op jit(solution)/shard_map/ppermute | solution.py:975
  362.4 9.2 %collective-permute-start.38 = (bf16[448,256]{1,0:T(8,128)(2,1)}, bf16[448,256]{1,0:T(8,128)(2,1)S(1)}, u32[]{:S(2)}, u32[]{:S(2)}) collective-permute-start(bf16[448,256]{1,0:T(8,128)(2,1)} %get-tuple-element.153), channel_id=1, source_target_pairs={{0,5},{1,4},{2,7},{3,6},{4,1},{5,0},{6,3},{7,2},{8,13},{9,12},{10,... | collective-permute-start | bytes 688136 | tf_op jit(solution)/shard_map/ppermute | solution.py:975
  366.4 10.9 %collective-permute-start.39 = (bf16[448,256]{1,0:T(8,128)(2,1)}, bf16[448,256]{1,0:T(8,128)(2,1)S(1)}, u32[]{:S(2)}, u32[]{:S(2)}) collective-permute-start(bf16[448,256]{1,0:T(8,128)(2,1)} %get-tuple-element.154), channel_id=1, source_target_pairs={{0,6},{1,7},{2,4},{3,5},{4,2},{5,3},{6,0},{7,1},{8,14},{9,15},{10,... | collective-permute-start | bytes 688136 | tf_op jit(solution)/shard_map/ppermute | solution.py:975
  366.9 14.4 %collective-permute-start.40 = (bf16[448,256]{1,0:T(8,128)(2,1)S(1)}, bf16[448,256]{1,0:T(8,128)(2,1)S(1)}, u32[]{:S(2)}, u32[]{:S(2)}) collective-permute-start(bf16[448,256]{1,0:T(8,128)(2,1)S(1)} %copy-done.49), channel_id=1, source_target_pairs={{0,7},{1,6},{2,5},{3,4},{4,3},{5,2},{6,1},{7,0},{8,15},{9,14},{10,... | collective-permute-start | bytes 688136 | tf_op jit(solution)/shard_map/ppermute | solution.py:975
  371.6 16.2 %collective-permute-start.29 = (bf16[464,256]{1,0:T(8,128)(2,1)S(1)}, bf16[464,256]{1,0:T(8,128)(2,1)S(1)}, u32[]{:S(2)}, u32[]{:S(2)}) collective-permute-start(bf16[464,256]{1,0:T(8,128)(2,1)S(1)} %copy-done.46), channel_id=1, source_target_pairs={{0,3},{1,2},{2,1},{3,0},{4,7},{5,6},{6,5},{7,4},{8,11},{9,10},{10,... | collective-permute-start | bytes 712712 | tf_op jit(solution)/shard_map/ppermute | solution.py:975
  377.2 10.5 %collective-permute-start.30 = (bf16[464,256]{1,0:T(8,128)(2,1)S(1)}, bf16[464,256]{1,0:T(8,128)(2,1)S(1)}, u32[]{:S(2)}, u32[]{:S(2)}) collective-permute-start(bf16[464,256]{1,0:T(8,128)(2,1)S(1)} %copy-done.45), channel_id=1, source_target_pairs={{0,4},{1,5},{2,6},{3,7},{4,0},{5,1},{6,2},{7,3},{8,12},{9,13},{10,... | collective-permute-start | bytes 712712 | tf_op jit(solution)/shard_map/ppermute | solution.py:975
  381.3 20.6 %collective-permute-start.31 = (bf16[464,256]{1,0:T(8,128)(2,1)S(1)}, bf16[464,256]{1,0:T(8,128)(2,1)S(1)}, u32[]{:S(2)}, u32[]{:S(2)}) collective-permute-start(bf16[464,256]{1,0:T(8,128)(2,1)S(1)} %copy-done.44), channel_id=1, source_target_pairs={{0,5},{1,4},{2,7},{3,6},{4,1},{5,0},{6,3},{7,2},{8,13},{9,12},{10,... | collective-permute-start | bytes 712712 | tf_op jit(solution)/shard_map/ppermute | solution.py:975
  383.1 18.8 %collective-permute-start.32 = (bf16[464,256]{1,0:T(8,128)(2,1)S(1)}, bf16[464,256]{1,0:T(8,128)(2,1)S(1)}, u32[]{:S(2)}, u32[]{:S(2)}) collective-permute-start(bf16[464,256]{1,0:T(8,128)(2,1)S(1)} %copy-done.43), channel_id=1, source_target_pairs={{0,6},{1,7},{2,4},{3,5},{4,2},{5,3},{6,0},{7,1},{8,14},{9,15},{10,... | collective-permute-start | bytes 712712 | tf_op jit(solution)/shard_map/ppermute | solution.py:975
  383.8 18.2 %collective-permute-start.33 = (bf16[464,256]{1,0:T(8,128)(2,1)S(1)}, bf16[464,256]{1,0:T(8,128)(2,1)S(1)}, u32[]{:S(2)}, u32[]{:S(2)}) collective-permute-start(bf16[464,256]{1,0:T(8,128)(2,1)S(1)} %copy-done.42), channel_id=1, source_target_pairs={{0,7},{1,6},{2,5},{3,4},{4,3},{5,2},{6,1},{7,0},{8,15},{9,14},{10,... | collective-permute-start | bytes 712712 | tf_op jit(solution)/shard_map/ppermute | solution.py:975
  (62 other events, 1534.5 us)
